TPU v7x, 256 devices: a whole 4x4x8 slice. The times are simulated.
256 devices in a mesh: seq: 128 (over x, y, z), head: 2 (over core).
Axes of the slice: x: 4, y: 4, z: 8, core: 2. Of those that a mesh axis runs over, the one named last changes fastest.
Arguments:
- query_rows: bfloat16 [131072, 16, 128], P('seq', 'head'), may hold values from -1.796875 to 1.796875
- key_rows: bfloat16 [131072, 16, 128], P('seq', 'head'), may hold values from -1.796875 to 1.796875
- value_rows: bfloat16 [131072, 16, 128], P('seq', 'head'), may hold values from -6 to 6
- level_codes: int32 [16, 18, 131072], P('head', None, 'seq'), may hold values from 0 to 63
- norm_gain: float32 [16, 128], P('head'), may hold values from 0.1 to 1.9
Outputs:
- normed: bfloat16 [131072, 16, 128], P('seq', 'head')
All inputs are finite; a program needn't handle non-finite values.
Results may differ from a plain program's by a relative error of at most 0.0022.
Values sent between devices are 32-bit elements; how exact they have to be, the bound alone decides.
No kernel may reach another device: no remote copies, remote signals or barrier semaphores. Data moves between devices by JAX's collectives and lax.ppermute only.
A program may use at most 128 MiB of HBM per device.

v0:
```python
import jax
import jax.numpy as jnp
import numpy as np
from jax import lax
from jax.sharding import PartitionSpec as P


def swapped(block, axis, stride):
    count = lax.axis_size(axis)
    route = []
    for low in range(count):
        high = low | 1 << stride
        if high != low and high < count:
            route += [(low, high), (high, low)]
    return lax.ppermute(block, axis, route)


def level_table(length_dev):
    target = np.arange(length_dev)[:, None]
    source = np.arange(length_dev)[None, :]
    levels = np.zeros((length_dev, length_dev), np.int32)
    for shift_count in range(24):
        levels = levels + (target >> shift_count != source >> shift_count).astype(np.int32)
    return levels


def attend_scores(query_head, key_head, value_head, weight_head, level_map, causal, local_bits):
    scores = jnp.dot(query_head, key_head.T, preferred_element_type=jnp.float32)
    picked = jnp.zeros(scores.shape, jnp.float32)
    for level in range(local_bits + 1):
        picked = jnp.where(level_map == level, weight_head[level][:, None], picked)
    weighted = jnp.where(causal, picked * scores, 0.0).astype(jnp.bfloat16)
    return jnp.dot(weighted, value_head, preferred_element_type=jnp.float32)


def local_heads(query_rows, key_rows, value_rows, weights, level_map, causal, local_bits):

    def per_head(inputs):
        result = attend_scores(
            inputs[0], inputs[1], inputs[2], inputs[3], level_map, causal, local_bits
        )
        key_state = jnp.dot(inputs[1].T, inputs[2], preferred_element_type=jnp.float32)
        return (result, key_state)

    results, states = lax.map(
        per_head,
        (
            jnp.swapaxes(query_rows, 0, 1),
            jnp.swapaxes(key_rows, 0, 1),
            jnp.swapaxes(value_rows, 0, 1),
            weights,
        ),
    )
    return (jnp.swapaxes(results, 0, 1), states)


def swap_together(states, level_bits):
    buckets = []
    block_sum = states
    for level_bit in range(level_bits):
        partner_sum = swapped(block_sum, "seq", level_bit)
        buckets.append(partner_sum)
        block_sum = block_sum + partner_sum
    return buckets


def read_levels(query_rows, buckets, weights, local_bits, position):
    query_wide = query_rows.astype(jnp.float32)
    cross_part = jnp.zeros(query_rows.shape, jnp.float32)
    for level_bit in range(len(buckets)):
        product = jnp.einsum(
            "thd,hde->the", query_wide, buckets[level_bit], precision=lax.Precision.HIGHEST
        )
        bit_flag = (position >> level_bit & 1).astype(jnp.float32)
        level_scale = weights[:, local_bits + 1 + level_bit, :].T
        cross_part = cross_part + (bit_flag * level_scale)[:, :, None] * product
    return cross_part


def shards(query_rows, key_rows, value_rows, level_codes, norm_gain):
    row_count = query_rows.shape[0]
    local_bits = row_count.bit_length() - 1
    level_bits = lax.axis_size("seq").bit_length() - 1
    position = lax.axis_index("seq")
    level_map = jnp.asarray(level_table(row_count))
    causal = jnp.asarray(np.tril(np.ones((row_count, row_count), np.int32)) > 0)
    weights = level_codes.astype(jnp.float32) / 64.0
    local_part, states = local_heads(
        query_rows, key_rows, value_rows, weights, level_map, causal, local_bits
    )
    buckets = swap_together(states, level_bits)
    result = local_part + read_levels(query_rows, buckets, weights, local_bits, position)
    mean_square = jnp.mean(result * result, axis=-1, keepdims=True)
    return (result * lax.rsqrt(mean_square + 1e-06) * norm_gain[None]).astype(jnp.bfloat16)


def solution(mesh):
    return jax.shard_map(
        shards,
        mesh=mesh,
        in_specs=(
            P("seq", "head", None),
            P("seq", "head", None),
            P("seq", "head", None),
            P("head", None, "seq"),
            P("head", None),
        ),
        out_specs=P("seq", "head", None),
        check_vma=False,
    )
```

profile of v0, /device:TPU:30, one launch (start us, length us, event | category | flops | bytes accessed | tf_op | source)
XLA Modules:
  0.0 249.9 jit_solution(5469674621800231816)
XLA Ops:
  0.0 0.0 copy-start.1
  0.0 0.0 copy-start.2
  0.0 1.6 fusion.29
  1.6 3.2 %copy.64 = bf16[1024,8,128]{2,0,1:T(8,128)(2,1)} copy(bf16[1024,8,128]{2,1,0:T(8,128)(2,1)} %param.9) | data formatting | bytes 4194304 | tf_op args[0]
  4.8 0.0 copy-done.1
  4.8 0.0 copy-done.2
  4.8 2.1 copy_bitcast_fusion
  6.9 106.2 %while.13 = (s32[]{:T(128)}, f32[8,1024,128]{1,2,0:T(8,128)}, f32[8,128,128]{1,2,0:T(8,128)}, f32[8,18,1024]{2,1,0:T(8,128)S(1)}, bf16[8,1024,128]{2,1,0:T(8,128...) while((s32[]{:T(128)}, f32[8,1024,128]{1,2,0:T(8,128)}, ...), condition=%wide.region_1.2_spmd.clone, body=%wide.region_0.1_spmd.sunk.clone.sunk | while | flops 585105408 | bytes 14622649 | solution.py:45
  7.0 1.9 fusion.63
  8.8 11.4 %fusion.62 = f32[8,1024,128]{1,2,0:T(8,128)} fusion(f32[8,1024,128]{1,2,0:T(8,128)} %get-tuple-element.220, s32[]{:T(128)S(6)} %copy.71, pred[1024,1024]{1,0:T(32,128)(4,1)} %get-tuple-element.258, pred[1024,1024]{1,0:T(32,128)(4,1)} %get-tuple-element.259, pred[1024,1024]{1,0:T(32,128)(4,1)} %get-tuple-element.260, ...), kind=kOutput, calls=%fused_computation.3.clone.1 | convolution fusion | flops 551550976 | bytes 13940736 | tf_op jit(solution)/shard_map/while/body/eval_jaxpr/dot_general | solution.py:33
  20.2 1.9 fusion.63
  22.1 11.4 %fusion.62 = f32[8,1024,128]{1,2,0:T(8,128)} fusion(f32[8,1024,128]{1,2,0:T(8,128)} %get-tuple-element.220, s32[]{:T(128)S(6)} %copy.71, pred[1024,1024]{1,0:T(32,128)(4,1)} %get-tuple-element.258, pred[1024,1024]{1,0:T(32,128)(4,1)} %get-tuple-element.259, pred[1024,1024]{1,0:T(32,128)(4,1)} %get-tuple-element.260, ...), kind=kOutput, calls=%fused_computation.3.clone.1 | convolution fusion | flops 551550976 | bytes 13940736 | tf_op jit(solution)/shard_map/while/body/eval_jaxpr/dot_general | solution.py:33
  33.5 1.9 fusion.63
  35.4 11.4 %fusion.62 = f32[8,1024,128]{1,2,0:T(8,128)} fusion(f32[8,1024,128]{1,2,0:T(8,128)} %get-tuple-element.220, s32[]{:T(128)S(6)} %copy.71, pred[1024,1024]{1,0:T(32,128)(4,1)} %get-tuple-element.258, pred[1024,1024]{1,0:T(32,128)(4,1)} %get-tuple-element.259, pred[1024,1024]{1,0:T(32,128)(4,1)} %get-tuple-element.260, ...), kind=kOutput, calls=%fused_computation.3.clone.1 | convolution fusion | flops 551550976 | bytes 13940736 | tf_op jit(solution)/shard_map/while/body/eval_jaxpr/dot_general | solution.py:33
  46.8 1.9 fusion.63
  48.7 11.4 %fusion.62 = f32[8,1024,128]{1,2,0:T(8,128)} fusion(f32[8,1024,128]{1,2,0:T(8,128)} %get-tuple-element.220, s32[]{:T(128)S(6)} %copy.71, pred[1024,1024]{1,0:T(32,128)(4,1)} %get-tuple-element.258, pred[1024,1024]{1,0:T(32,128)(4,1)} %get-tuple-element.259, pred[1024,1024]{1,0:T(32,128)(4,1)} %get-tuple-element.260, ...), kind=kOutput, calls=%fused_computation.3.clone.1 | convolution fusion | flops 551550976 | bytes 13940736 | tf_op jit(solution)/shard_map/while/body/eval_jaxpr/dot_general | solution.py:33
  60.1 1.9 fusion.63
  62.0 11.4 %fusion.62 = f32[8,1024,128]{1,2,0:T(8,128)} fusion(f32[8,1024,128]{1,2,0:T(8,128)} %get-tuple-element.220, s32[]{:T(128)S(6)} %copy.71, pred[1024,1024]{1,0:T(32,128)(4,1)} %get-tuple-element.258, pred[1024,1024]{1,0:T(32,128)(4,1)} %get-tuple-element.259, pred[1024,1024]{1,0:T(32,128)(4,1)} %get-tuple-element.260, ...), kind=kOutput, calls=%fused_computation.3.clone.1 | convolution fusion | flops 551550976 | bytes 13940736 | tf_op jit(solution)/shard_map/while/body/eval_jaxpr/dot_general | solution.py:33
  73.4 1.9 fusion.63
  75.2 11.4 %fusion.62 = f32[8,1024,128]{1,2,0:T(8,128)} fusion(f32[8,1024,128]{1,2,0:T(8,128)} %get-tuple-element.220, s32[]{:T(128)S(6)} %copy.71, pred[1024,1024]{1,0:T(32,128)(4,1)} %get-tuple-element.258, pred[1024,1024]{1,0:T(32,128)(4,1)} %get-tuple-element.259, pred[1024,1024]{1,0:T(32,128)(4,1)} %get-tuple-element.260, ...), kind=kOutput, calls=%fused_computation.3.clone.1 | convolution fusion | flops 551550976 | bytes 13940736 | tf_op jit(solution)/shard_map/while/body/eval_jaxpr/dot_general | solution.py:33
  86.6 1.9 fusion.63
  88.5 11.4 %fusion.62 = f32[8,1024,128]{1,2,0:T(8,128)} fusion(f32[8,1024,128]{1,2,0:T(8,128)} %get-tuple-element.220, s32[]{:T(128)S(6)} %copy.71, pred[1024,1024]{1,0:T(32,128)(4,1)} %get-tuple-element.258, pred[1024,1024]{1,0:T(32,128)(4,1)} %get-tuple-element.259, pred[1024,1024]{1,0:T(32,128)(4,1)} %get-tuple-element.260, ...), kind=kOutput, calls=%fused_computation.3.clone.1 | convolution fusion | flops 551550976 | bytes 13940736 | tf_op jit(solution)/shard_map/while/body/eval_jaxpr/dot_general | solution.py:33
  99.9 1.8 fusion.63
  101.7 11.4 %fusion.62 = f32[8,1024,128]{1,2,0:T(8,128)} fusion(f32[8,1024,128]{1,2,0:T(8,128)} %get-tuple-element.220, s32[]{:T(128)S(6)} %copy.71, pred[1024,1024]{1,0:T(32,128)(4,1)} %get-tuple-element.258, pred[1024,1024]{1,0:T(32,128)(4,1)} %get-tuple-element.259, pred[1024,1024]{1,0:T(32,128)(4,1)} %get-tuple-element.260, ...), kind=kOutput, calls=%fused_computation.3.clone.1 | convolution fusion | flops 551550976 | bytes 13940736 | tf_op jit(solution)/shard_map/while/body/eval_jaxpr/dot_general | solution.py:33
  113.1 0.0 copy-start.5
  113.1 0.9 copy-done.5
  114.0 0.0 copy-start
  114.0 1.9 collective-permute-start
  115.9 12.1 %collective-permute-done = f32[8,128,128]{1,2,0:T(8,128)S(1)} collective-permute-done((f32[8,128,128]{1,2,0:T(8,128)}, f32[8,128,128]{1,2,0:T(8,128)S(1)}, u32[]{:S(2)}, u32[]{:S(2)}) %collective-permute-start) | collective-permute-done | bytes 524320 | tf_op jit(solution)/shard_map/ppermute | solution.py:15
  128.1 1.1 add.53
  129.2 3.4 %collective-permute-start.1 = (f32[8,128,128]{1,2,0:T(8,128)S(1)}, f32[8,128,128]{1,2,0:T(8,128)S(1)}, u32[]{:S(2)}, u32[]{:S(2)}) collective-permute-start(f32[8,128,128]{1,2,0:T(8,128)S(1)} %add.53), channel_id=1, source_target_pairs={{0,4},{4,0},{2,6},{6,2},{8,12},{12,8},{10,14},{14,10},{16,20},{20,... | collective-permute-start | bytes 1572872 | tf_op jit(solution)/shard_map/ppermute | solution.py:15
  132.5 22.5 %collective-permute-done.1 = f32[8,128,128]{1,2,0:T(8,128)S(1)} collective-permute-done((f32[8,128,128]{1,2,0:T(8,128)S(1)}, f32[8,128,128]{1,2,0:T(8,128)S(1)}, u32[]{:S(2)}, u32[]{:S(2)}) %collective-permute-start.1) | collective-permute-done | bytes 524320 | tf_op jit(solution)/shard_map/ppermute | solution.py:15
  155.0 0.0 copy-start.3
  155.0 0.1 add.55
  155.0 0.7 copy-done.3
  155.8 6.2 %collective-permute-start.2 = (f32[8,128,128]{1,2,0:T(8,128)S(1)}, f32[8,128,128]{1,2,0:T(8,128)}, u32[]{:S(2)}, u32[]{:S(2)}) collective-permute-start(f32[8,128,128]{1,2,0:T(8,128)S(1)} %add.55), channel_id=1, source_target_pairs={{0,8},{8,0},{2,10},{10,2},{4,12},{12,4},{6,14},{14,6},{16,24},{24,... | collective-permute-start | bytes 1572872 | tf_op jit(solution)/shard_map/ppermute | solution.py:15
  162.0 2.0 slice_multiply_fusion.6
  163.9 21.1 %collective-permute-done.2 = f32[8,128,128]{1,2,0:T(8,128)} collective-permute-done((f32[8,128,128]{1,2,0:T(8,128)S(1)}, f32[8,128,128]{1,2,0:T(8,128)}, u32[]{:S(2)}, u32[]{:S(2)}) %collective-permute-start.2) | collective-permute-done | bytes 524320 | tf_op jit(solution)/shard_map/ppermute | solution.py:15
  185.1 1.1 add.57
  186.2 0.8 collective-permute-start.3
  187.1 0.0 copy-start.4
  187.1 11.8 %collective-permute-done.3 = f32[8,128,128]{1,2,0:T(8,128)S(1)} collective-permute-done((f32[8,128,128]{1,2,0:T(8,128)S(1)}, f32[8,128,128]{1,2,0:T(8,128)S(1)}, u32[]{:S(2)}, u32[]{:S(2)}) %collective-permute-start.3) | collective-permute-done | bytes 524320 | tf_op jit(solution)/shard_map/ppermute | solution.py:15
  198.9 0.1 add.59
  199.0 1.5 collective-permute-start.4
  200.5 0.0 copy-done
  200.5 1.8 fusion.41
  202.4 0.0 copy-done.4
  202.4 3.8 %fusion.39 = f32[8,128,1024]{2,1,0:T(8,128)} fusion(f32[8,128,128]{1,2,0:T(8,128)S(1)} %copy-done.4, bf16[1024,8,128]{2,1,0:T(8,128)(2,1)S(1)} %copy-done), kind=kOutput, calls=%fused_computation.59 | convolution fusion | flops 1610612736 | bytes 6815744 | tf_op jit(solution)/shard_map/thd,hde->the/dot_general | solution.py:71
  206.2 6.4 %collective-permute-done.4 = f32[8,128,128]{1,2,0:T(8,128)S(1)} collective-permute-done((f32[8,128,128]{1,2,0:T(8,128)S(1)}, f32[8,128,128]{1,2,0:T(8,128)S(1)}, u32[]{:S(2)}, u32[]{:S(2)}) %collective-permute-start.4) | collective-permute-done | bytes 524320 | tf_op jit(solution)/shard_map/ppermute | solution.py:15
  212.5 0.1 add.61
  212.6 0.9 collective-permute-start.5
  213.5 4.9 %fusion.37 = f32[8,128,1024]{2,1,0:T(8,128)} fusion(f32[8,128,128]{1,2,0:T(8,128)} %collective-permute-done.2, bf16[1024,8,128]{2,1,0:T(8,128)(2,1)S(1)} %copy-done), kind=kOutput, calls=%fused_computation.57 | convolution fusion | flops 1610612736 | bytes 6815744 | tf_op jit(solution)/shard_map/thd,hde->the/dot_general | solution.py:71
  218.3 3.8 %fusion.35 = f32[8,128,1024]{2,1,0:T(8,128)} fusion(f32[8,128,128]{1,2,0:T(8,128)S(1)} %collective-permute-done.3, bf16[1024,8,128]{2,1,0:T(8,128)(2,1)S(1)} %copy-done), kind=kOutput, calls=%fused_computation.55 | convolution fusion | flops 1610612736 | bytes 6815744 | tf_op jit(solution)/shard_map/thd,hde->the/dot_general | solution.py:71
  222.1 3.0 %collective-permute-done.5 = f32[8,128,128]{1,2,0:T(8,128)S(1)} collective-permute-done((f32[8,128,128]{1,2,0:T(8,128)S(1)}, f32[8,128,128]{1,2,0:T(8,128)S(1)}, u32[]{:S(2)}, u32[]{:S(2)}) %collective-permute-start.5) | collective-permute-done | bytes 524320 | tf_op jit(solution)/shard_map/ppermute | solution.py:15
  225.2 0.1 add.63
  225.2 0.3 collective-permute-start.6
  225.5 3.8 %fusion.33 = f32[8,128,1024]{2,1,0:T(8,128)} fusion(f32[8,128,128]{1,2,0:T(8,128)S(1)} %collective-permute-done.4, bf16[1024,8,128]{2,1,0:T(8,128)(2,1)S(1)} %copy-done), kind=kOutput, calls=%fused_computation.53 | convolution fusion | flops 1610612736 | bytes 6815744 | tf_op jit(solution)/shard_map/thd,hde->the/dot_general | solution.py:71
  229.3 3.8 %fusion.31 = f32[8,128,1024]{2,1,0:T(8,128)} fusion(f32[8,128,128]{1,2,0:T(8,128)S(1)} %collective-permute-done.5, bf16[1024,8,128]{2,1,0:T(8,128)(2,1)S(1)} %copy-done), kind=kOutput, calls=%fused_computation.51 | convolution fusion | flops 1610612736 | bytes 6815744 | tf_op jit(solution)/shard_map/thd,hde->the/dot_general | solution.py:71
  233.1 3.1 %collective-permute-done.6 = f32[8,128,128]{1,2,0:T(8,128)S(1)} collective-permute-done((f32[8,128,128]{1,2,0:T(8,128)S(1)}, f32[8,128,128]{1,2,0:T(8,128)S(1)}, u32[]{:S(2)}, u32[]{:S(2)}) %collective-permute-start.6) | collective-permute-done | bytes 524320 | tf_op jit(solution)/shard_map/ppermute | solution.py:15
  236.2 0.0 copy-start.6
  236.2 10.3 %multiply_reduce_fusion = (f32[1024,8]{0,1:T(8,128)S(1)}, f32[1024,8,128]{0,2,1:T(8,128)S(1)}) fusion(f32[8,128,128]{1,2,0:T(8,128)S(1)} %collective-permute-done.6, bf16[1024,8,128]{2,1,0:T(8,128)(2,1)S(1)} %copy-done, f32[1024,8]{0,1:T(8,128)S(1)} %get-tuple-element.117, f32[8,128,1024]{2,1,0:T(8,128)} %fusion.31, f32[1024,8]{0,1:T(8,128)S(1)} %get-tuple-element.118, ...), kind=kOutput, calls=%fused_computation.45 | convolution fusion | flops 1627381760 | bytes 36438016 | tf_op jit(solution)/shard_map/thd,hde->the/dot_general | solution.py:71
  246.6 0.0 copy-done.6
  246.6 0.5 multiply_convert_fusion
  247.0 2.9 %copy.22 = bf16[1024,8,128]{2,1,0:T(8,128)(2,1)} copy(bf16[1024,8,128]{0,2,1:T(8,128)(2,1)S(1)} %multiply_convert_fusion) | data formatting | bytes 4194304 | tf_op jit(solution)/shard_map/convert_element_type | solution.py:94
  (15 shorter events, 0.4 us)
Async XLA Ops:
  0.0 4.8 %copy-start.1 = (bf16[1024,8,128]{2,1,0:T(8,128)(2,1)S(1)}, bf16[1024,8,128]{2,1,0:T(8,128)(2,1)}, u32[]{:S(2)}) copy-start(bf16[1024,8,128]{2,1,0:T(8,128)(2,1)} %param.11) | copy-start | bytes 6291460
  0.0 4.8 %copy-start.2 = (bf16[1024,8,128]{2,1,0:T(8,128)(2,1)S(1)}, bf16[1024,8,128]{2,1,0:T(8,128)(2,1)}, u32[]{:S(2)}) copy-start(bf16[1024,8,128]{2,1,0:T(8,128)(2,1)} %param.10) | copy-start | bytes 6291460
  113.1 0.9 copy-start.5
  114.0 86.5 %copy-start = (bf16[1024,8,128]{2,1,0:T(8,128)(2,1)S(1)}, bf16[1024,8,128]{2,1,0:T(8,128)(2,1)}, u32[]{:S(2)}) copy-start(bf16[1024,8,128]{2,1,0:T(8,128)(2,1)} %param.9) | copy-start | bytes 6291460
  114.0 14.1 %collective-permute-start = (f32[8,128,128]{1,2,0:T(8,128)}, f32[8,128,128]{1,2,0:T(8,128)S(1)}, u32[]{:S(2)}, u32[]{:S(2)}) collective-permute-start(f32[8,128,128]{1,2,0:T(8,128)} %get-tuple-element.54), channel_id=1, source_target_pairs={{0,2},{2,0},{4,6},{6,4},{8,10},{10,8},{12,14},{14,12},{16,18},{18,... | collective-permute-start | bytes 1572872 | tf_op jit(solution)/shard_map/ppermute | solution.py:15
  129.2 25.8 %collective-permute-start.1 = (f32[8,128,128]{1,2,0:T(8,128)S(1)}, f32[8,128,128]{1,2,0:T(8,128)S(1)}, u32[]{:S(2)}, u32[]{:S(2)}) collective-permute-start(f32[8,128,128]{1,2,0:T(8,128)S(1)} %add.53), channel_id=1, source_target_pairs={{0,4},{4,0},{2,6},{6,2},{8,12},{12,8},{10,14},{14,10},{16,20},{20,... | collective-permute-start | bytes 1572872 | tf_op jit(solution)/shard_map/ppermute | solution.py:15
  155.0 0.8 copy-start.3
  155.8 29.3 %collective-permute-start.2 = (f32[8,128,128]{1,2,0:T(8,128)S(1)}, f32[8,128,128]{1,2,0:T(8,128)}, u32[]{:S(2)}, u32[]{:S(2)}) collective-permute-start(f32[8,128,128]{1,2,0:T(8,128)S(1)} %add.55), channel_id=1, source_target_pairs={{0,8},{8,0},{2,10},{10,2},{4,12},{12,4},{6,14},{14,6},{16,24},{24,... | collective-permute-start | bytes 1572872 | tf_op jit(solution)/shard_map/ppermute | solution.py:15
  186.2 12.8 %collective-permute-start.3 = (f32[8,128,128]{1,2,0:T(8,128)S(1)}, f32[8,128,128]{1,2,0:T(8,128)S(1)}, u32[]{:S(2)}, u32[]{:S(2)}) collective-permute-start(f32[8,128,128]{1,2,0:T(8,128)S(1)} %add.57), channel_id=1, source_target_pairs={{0,16},{16,0},{2,18},{18,2},{4,20},{20,4},{6,22},{22,6},{8,24},{24... | collective-permute-start | bytes 1572872 | tf_op jit(solution)/shard_map/ppermute | solution.py:15
  187.1 15.3 %copy-start.4 = (f32[8,128,128]{1,2,0:T(8,128)S(1)}, f32[8,128,128]{1,2,0:T(8,128)}, u32[]{:S(2)}) copy-start(f32[8,128,128]{1,2,0:T(8,128)} %copy-done.3) | copy-start | bytes 1572868
  199.0 13.5 %collective-permute-start.4 = (f32[8,128,128]{1,2,0:T(8,128)S(1)}, f32[8,128,128]{1,2,0:T(8,128)S(1)}, u32[]{:S(2)}, u32[]{:S(2)}) collective-permute-start(f32[8,128,128]{1,2,0:T(8,128)S(1)} %add.59), channel_id=1, source_target_pairs={{0,32},{32,0},{2,34},{34,2},{4,36},{36,4},{6,38},{38,6},{8,40},{40... | collective-permute-start | bytes 1572872 | tf_op jit(solution)/shard_map/ppermute | solution.py:15
  212.6 12.5 %collective-permute-start.5 = (f32[8,128,128]{1,2,0:T(8,128)S(1)}, f32[8,128,128]{1,2,0:T(8,128)S(1)}, u32[]{:S(2)}, u32[]{:S(2)}) collective-permute-start(f32[8,128,128]{1,2,0:T(8,128)S(1)} %add.61), channel_id=1, source_target_pairs={{0,64},{64,0},{2,66},{66,2},{4,68},{68,4},{6,70},{70,6},{8,72},{72... | collective-permute-start | bytes 1572872 | tf_op jit(solution)/shard_map/ppermute | solution.py:15
  225.2 11.0 %collective-permute-start.6 = (f32[8,128,128]{1,2,0:T(8,128)S(1)}, f32[8,128,128]{1,2,0:T(8,128)S(1)}, u32[]{:S(2)}, u32[]{:S(2)}) collective-permute-start(f32[8,128,128]{1,2,0:T(8,128)S(1)} %add.63), channel_id=1, source_target_pairs={{0,128},{128,0},{2,130},{130,2},{4,132},{132,4},{6,134},{134,6},{8... | collective-permute-start | bytes 1572872 | tf_op jit(solution)/shard_map/ppermute | solution.py:15
  236.2 10.4 %copy-start.6 = (f32[8,128]{1,0:T(8,128)S(1)}, f32[8,128]{1,0:T(8,128)}, u32[]{:S(2)}) copy-start(f32[8,128]{1,0:T(8,128)} %param.13) | copy-start | bytes 12292
where the time goes:
time: 252 us; the launch traced here: 250 us
  matrix products  138 us (55%)
  waiting for transfers between devices  80.1 us (32%)
  starting transfers between devices  15 us (6%)
  local copies, waits for them, and re-layouts  10.2 us (4%)
  other arithmetic  6.48 us (3%)
    dot_general x8, matrix products, attend_scores(): return jnp.dot(weighted, value_head, preferred_element_type=jnp.float32)  91 us
    ppermute x7, waiting for transfers between devices, swapped(): return lax.ppermute(block, axis, route)  80.1 us
    dot_general x7, matrix products, read_levels(): jnp.einsum('thd,hde->the', query_wide, buckets[level_bit], precision=lax....  32.2 us
    ppermute x7, starting transfers between devices, swapped(): return lax.ppermute(block, axis, route)  15 us
    dot_general x8, matrix products, per_head(): jnp.dot(inputs[1].T, inputs[2], preferred_element_type=jnp.float32)  14.8 us
  transfers between devices with their start and end apart: 7, of which 7 were waited for; matrix products, arithmetic and copies ran while one was open for 10% of the time, Pallas kernels for 0%

commit v1 on v0

v1 whole, which is shorter than its diff:
```python
import functools

import jax
import jax.numpy as jnp
import numpy as np
from jax import lax
from jax.experimental import pallas as pl
from jax.experimental.pallas import tpu as pltpu
from jax.sharding import PartitionSpec as P

VMEM_LIMIT = 40 * 1024 * 1024
NT = (((1,), (1,)), ((), ()))


def params():
    return pltpu.CompilerParams(vmem_limit_bytes=VMEM_LIMIT)


def cost(flops, nbytes):
    return pl.CostEstimate(flops=flops, bytes_accessed=nbytes, transcendentals=0)


def level_map(size):
    source = np.arange(size)[:, None]
    target = np.arange(size)[None, :]
    levels = np.zeros((size, size), np.int32)
    for shift in range(24):
        levels += (target >> shift != source >> shift).astype(np.int32)
    return np.where(source <= target, levels, -1).astype(np.int32)


def states_kernel(heads, rows, k_ref, v_ref, key_out, value_out, state_out, k_wide, v_wide):
    k_wide[...] = k_ref[...].astype(jnp.float32)
    v_wide[...] = v_ref[...].astype(jnp.float32)

    @pl.when(pl.program_id(0) == 0)
    def _():
        state_out[...] = jnp.zeros_like(state_out)

    for h in range(heads):
        key = k_wide[pl.ds(h, rows, stride=heads), :].astype(jnp.bfloat16)
        value = v_wide[pl.ds(h, rows, stride=heads), :].T.astype(jnp.bfloat16)
        key_out[h] = key
        value_out[h] = value
        state_out[h] += jnp.dot(value, key, preferred_element_type=jnp.float32)


def make_states(key_rows, value_rows, rows=256):
    length, heads, dim = key_rows.shape
    flat = pl.BlockSpec((rows * heads, dim), lambda i: (i, 0))
    return pl.pallas_call(
        functools.partial(states_kernel, heads, rows),
        grid=(length // rows,),
        in_specs=[flat, flat],
        out_specs=[
            pl.BlockSpec((heads, rows, dim), lambda i: (0, i, 0)),
            pl.BlockSpec((heads, dim, rows), lambda i: (0, 0, i)),
            pl.BlockSpec((heads, dim, dim), lambda i: (0, 0, 0)),
        ],
        out_shape=[
            jax.ShapeDtypeStruct((heads, length, dim), jnp.bfloat16),
            jax.ShapeDtypeStruct((heads, dim, length), jnp.bfloat16),
            jax.ShapeDtypeStruct((heads, dim, dim), jnp.float32),
        ],
        scratch_shapes=[pltpu.VMEM((rows * heads, dim), jnp.float32)] * 2,
        compiler_params=params(),
        cost_estimate=cost(2 * heads * length * dim * dim, 8 * length * heads * dim),
        name="states",
    )(key_rows.reshape(length * heads, dim), value_rows.reshape(length * heads, dim))


def split_kernel(heads, rows, q_ref, q_out, q_wide):
    q_wide[...] = q_ref[...].astype(jnp.float32)
    for h in range(heads):
        q_out[h] = q_wide[pl.ds(h, rows, stride=heads), :].astype(jnp.bfloat16)


def split_heads(query_rows, rows=256):
    length, heads, dim = query_rows.shape
    return pl.pallas_call(
        functools.partial(split_kernel, heads, rows),
        grid=(length // rows,),
        in_specs=[pl.BlockSpec((rows * heads, dim), lambda i: (i, 0))],
        out_specs=pl.BlockSpec((heads, rows, dim), lambda i: (0, i, 0)),
        out_shape=jax.ShapeDtypeStruct((heads, length, dim), jnp.bfloat16),
        scratch_shapes=[pltpu.VMEM((rows * heads, dim), jnp.float32)],
        compiler_params=params(),
        cost_estimate=cost(0, 4 * length * heads * dim),
        name="split_heads",
    )(query_rows.reshape(length * heads, dim))


def local_kernel(length, tile, small, q_ref, k_ref, v_ref, codes_ref, map_ref, out_ref):
    weights = codes_ref[0].astype(jnp.float32) * (1.0 / 64.0)
    low_levels = small.bit_length()
    levels = map_ref[...]
    masks = [levels == level for level in range(low_levels)]
    for t in range(length // tile):
        columns = slice(t * tile, (t + 1) * tile)
        count = (t + 1) * tile
        scores = lax.dot_general(
            k_ref[0, :count, :], q_ref[0, columns, :], NT, preferred_element_type=jnp.float32
        )
        pieces = []
        for s in range(t):
            level = (t ^ s).bit_length() + tile.bit_length() - 1
            piece = scores[s * tile:(s + 1) * tile] * weights[level:level + 1, columns]
            pieces.append(piece.astype(jnp.bfloat16))
        for i in range(tile // small):
            row = []
            for j in range(tile // small):
                first = t * tile + j * small
                lanes = slice(first, first + small)
                part = scores[t * tile + i * small:t * tile + (i + 1) * small, j * small:(j + 1) * small]
                if j < i:
                    row.append(jnp.zeros((small, small), jnp.bfloat16))
                    continue
                if j > i:
                    level = (i ^ j).bit_length() + small.bit_length() - 1
                    picked = weights[level:level + 1, lanes]
                else:
                    picked = jnp.zeros((small, small), jnp.float32)
                    for level in range(low_levels):
                        picked = jnp.where(masks[level], weights[level:level + 1, lanes], picked)
                row.append((part * picked).astype(jnp.bfloat16))
            pieces.append(jnp.concatenate(row, axis=1))
        weighted = jnp.concatenate(pieces, axis=0) if len(pieces) > 1 else pieces[0]
        out_ref[0, :, columns] = jnp.dot(
            v_ref[0, :, :count], weighted, preferred_element_type=jnp.float32
        )


def local_part(query, key, value, codes, tile=256, small=128):
    heads, length, dim = query.shape
    levels = codes.shape[1]
    return pl.pallas_call(
        functools.partial(local_kernel, length, tile, small),
        grid=(heads,),
        in_specs=[
            pl.BlockSpec((1, length, dim), lambda h: (h, 0, 0)),
            pl.BlockSpec((1, length, dim), lambda h: (h, 0, 0)),
            pl.BlockSpec((1, dim, length), lambda h: (h, 0, 0)),
            pl.BlockSpec((1, levels, length), lambda h: (h, 0, 0)),
            pl.BlockSpec((small, small), lambda h: (0, 0)),
        ],
        out_specs=pl.BlockSpec((1, dim, length), lambda h: (h, 0, 0)),
        out_shape=jax.ShapeDtypeStruct((heads, dim, length), jnp.float32),
        compiler_params=params(),
        cost_estimate=cost(16 * heads * length * length * dim, 16 * length * heads * dim),
        name="local_part",
    )(query, key, value, codes, jnp.asarray(level_map(small)))


def bucket_product(bucket, query):
    high = bucket.astype(jnp.bfloat16)
    low = (bucket - high.astype(jnp.float32)).astype(jnp.bfloat16)
    both = lax.dot_general(
        jnp.concatenate([high, low], axis=0), query, NT, preferred_element_type=jnp.float32
    )
    dim = bucket.shape[0]
    return both[:dim] + both[dim:]


def cross_kernel(bits, first, total_ref, q_ref, codes_ref, flag_ref, *refs):
    out_ref = refs[-1]
    total = total_ref[0]
    for bit, bucket_ref in zip(bits, refs[:-1]):
        scale = codes_ref[0, first + bit:first + bit + 1, :].astype(jnp.float32) * flag_ref[bit]
        total = total + scale * bucket_product(bucket_ref[0], q_ref[0])
    out_ref[0] = total


def add_cross(total, query, codes, flags, buckets, bits, first):
    heads, length, dim = query.shape
    levels = codes.shape[1]
    return pl.pallas_call(
        functools.partial(cross_kernel, bits, first),
        grid=(heads,),
        in_specs=[
            pl.BlockSpec((1, dim, length), lambda h: (h, 0, 0)),
            pl.BlockSpec((1, length, dim), lambda h: (h, 0, 0)),
            pl.BlockSpec((1, levels, length), lambda h: (h, 0, 0)),
            pl.BlockSpec(memory_space=pltpu.SMEM),
        ] + [pl.BlockSpec((1, dim, dim), lambda h: (h, 0, 0))] * len(bits),
        out_specs=pl.BlockSpec((1, dim, length), lambda h: (h, 0, 0)),
        out_shape=jax.ShapeDtypeStruct((heads, dim, length), jnp.float32),
        input_output_aliases={0: 0},
        compiler_params=params(),
        cost_estimate=cost(8 * len(bits) * heads * length * dim * dim, 12 * length * heads * dim),
        name="add_cross",
    )(total, query, codes, flags, *buckets)


def finish_kernel(bits, first, total_ref, q_ref, codes_ref, flag_ref, gain_ref, *refs):
    out_ref, wide = refs[-2:]
    heads, dim, rows = total_ref.shape
    for h in range(heads):
        total = total_ref[h]
        for bit, bucket_ref in zip(bits, refs[:-2]):
            scale = codes_ref[h, first + bit:first + bit + 1, :].astype(jnp.float32) * flag_ref[bit]
            total = total + scale * bucket_product(bucket_ref[h], q_ref[h])
        mean_square = jnp.sum(total * total, axis=0, keepdims=True) * (1.0 / dim)
        normed = total * lax.rsqrt(mean_square + 1e-06)
        wide[pl.ds(h, rows, stride=heads), :] = normed.T * gain_ref[h:h + 1, :]
    out_ref[...] = wide[...].astype(jnp.bfloat16)


def finish(total, query, codes, flags, gain, buckets, bits, first, rows=256):
    heads, length, dim = query.shape
    levels = codes.shape[1]
    out = pl.pallas_call(
        functools.partial(finish_kernel, bits, first),
        grid=(length // rows,),
        in_specs=[
            pl.BlockSpec((heads, dim, rows), lambda i: (0, 0, i)),
            pl.BlockSpec((heads, rows, dim), lambda i: (0, i, 0)),
            pl.BlockSpec((heads, levels, rows), lambda i: (0, 0, i)),
            pl.BlockSpec(memory_space=pltpu.SMEM),
            pl.BlockSpec((heads, dim), lambda i: (0, 0)),
        ] + [pl.BlockSpec((heads, dim, dim), lambda i: (0, 0, 0))] * len(bits),
        out_specs=pl.BlockSpec((rows * heads, dim), lambda i: (i, 0)),
        out_shape=jax.ShapeDtypeStruct((length * heads, dim), jnp.bfloat16),
        scratch_shapes=[pltpu.VMEM((rows * heads, dim), jnp.float32)],
        compiler_params=params(),
        cost_estimate=cost(8 * heads * length * dim * dim, 10 * length * heads * dim),
        name="finish",
    )(total, query, codes, flags, gain, *buckets)
    return out.reshape(length, heads, dim)


def swapped(block, mask):
    count = lax.axis_size("seq")
    return lax.ppermute(block, "seq", [(i, i ^ mask) for i in range(count)])


MASKS = (1, 3, 7, 8, 24, 32, 96)


def shards(query_rows, key_rows, value_rows, level_codes, norm_gain):
    first = level_codes.shape[1] - len(MASKS)
    position = lax.axis_index("seq")
    bits = jnp.arange(len(MASKS), dtype=jnp.int32)
    flags = (position >> bits & 1).astype(jnp.float32) * (1.0 / 64.0)
    key, value, states = make_states(key_rows, value_rows)
    buckets = []
    block_sum = states
    for mask in MASKS:
        partner = swapped(block_sum, mask)
        buckets.append(partner)
        block_sum = block_sum + partner
    query = split_heads(query_rows)
    total = local_part(query, key, value, level_codes)
    total = add_cross(total, query, level_codes, flags, buckets[:3], (0, 1, 2), first)
    total = add_cross(total, query, level_codes, flags, buckets[3:6], (3, 4, 5), first)
    return finish(total, query, level_codes, flags, norm_gain, buckets[6:], (6,), first)


def solution(mesh):
    return jax.shard_map(
        shards,
        mesh=mesh,
        in_specs=(
            P("seq", "head", None),
            P("seq", "head", None),
            P("seq", "head", None),
            P("head", None, "seq"),
            P("head", None),
        ),
        out_specs=P("seq", "head", None),
        check_vma=False,
    )
```

time: 252 us -> 124 us (0.49)
  the two profiles are of different devices: /device:TPU:30 before, /device:TPU:32 now
where the time goes in v1:
time: 124 us
  waiting for transfers between devices  62.8 us (51%)
  Pallas kernels  30.7 us (25%)
  starting transfers between devices  18 us (15%)
  local copies, waits for them, and re-layouts  9.78 us (8%)
  other arithmetic  2.48 us (2%)
    ppermute x7, waiting for transfers between devices, swapped(): return lax.ppermute(block, 'seq', [(i, i ^ mask) for i in range(count)])  62.8 us
    ppermute x7, starting transfers between devices, swapped(): return lax.ppermute(block, 'seq', [(i, i ^ mask) for i in range(count)])  18 us
    pallas_call x2, Pallas kernels, add_cross(): pl.pallas_call(functools.partial(cross_kernel, bits, first), grid=(heads,...  11.6 us
    pallas_call x1, Pallas kernels, local_part(): pl.pallas_call(functools.partial(local_kernel, length, tile, small), grid...  10.2 us
    unnamed x33, local copies, waits for them, and re-layouts  9.78 us
    pallas_call x1, Pallas kernels, finish(): pl.pallas_call(functools.partial(finish_kernel, bits, first), grid=(lengt...  4.62 us
    pallas_call x1, Pallas kernels, make_states(): pl.pallas_call(functools.partial(states_kernel, heads, rows), grid=(lengt...  3.07 us
  transfers between devices with their start and end apart: 7, of which 5 were waited for; matrix products, arithmetic and copies ran while one was open for 0% of the time, Pallas kernels for 19%

profile of v1, /device:TPU:32, one launch (start us, length us, event | category | flops | bytes accessed | tf_op | source)
XLA Modules:
  0.0 123.9 jit_solution(7417679216231841050)
XLA Ops:
  0.0 0.0 copy-start.10
  0.0 1.6 %copy-done.10 = bf16[1024,8,128]{2,1,0:T(8,128)(2,1)S(1)} copy-done((bf16[1024,8,128]{2,1,0:T(8,128)(2,1)S(1)}, bf16[1024,8,128]{2,1,0:T(8,128)(2,1)}, u32[]{:S(2)}) %copy-start.10) | copy-done | bytes 2097176
  1.6 0.0 copy-start.11
  1.6 1.6 %copy-done.11 = bf16[1024,8,128]{2,1,0:T(8,128)(2,1)S(1)} copy-done((bf16[1024,8,128]{2,1,0:T(8,128)(2,1)S(1)}, bf16[1024,8,128]{2,1,0:T(8,128)(2,1)}, u32[]{:S(2)}) %copy-start.11) | copy-done | bytes 2097176
  3.2 3.1 %states.1 = (bf16[8,1024,128]{2,1,0:T(8,128)(2,1)S(1)}, bf16[8,128,1024]{2,1,0:T(8,128)(2,1)S(1)}, f32[8,128,128]{2,1,0:T(8,128)S(1)}) custom-call(bf16[8192,128]{1,0:T(8,128)(2,1)S(1)} %bitcast.4, bf16[8192,128]{1,0:T(8,128)(2,1)S(1)} %bitcast.5), custom_call_target="tpu_custom_call" | custom-call | flops 268435456 | bytes 8388608 | tf_op jit(solution)/shard_map/states/pallas_call | solution.py:51
  6.3 1.9 %collective-permute-start = (f32[8,128,128]{2,1,0:T(8,128)S(1)}, f32[8,128,128]{2,1,0:T(8,128)S(1)}, u32[]{:S(2)}, u32[]{:S(2)}) collective-permute-start(f32[8,128,128]{2,1,0:T(8,128)S(1)} %get-tuple-element.10), channel_id=1, source_target_pairs={{0,2},{2,0},{4,6},{6,4},{8,10},{10,8},{12,14},{14,12},{16,18},{18,... | collective-permute-start | bytes 1572872 | tf_op jit(solution)/shard_map/ppermute | solution.py:233
  8.2 11.8 %collective-permute-done.refs_0_ = f32[8,128,128]{2,1,0:T(8,128)S(1)} collective-permute-done((f32[8,128,128]{2,1,0:T(8,128)S(1)}, f32[8,128,128]{2,1,0:T(8,128)S(1)}, u32[]{:S(2)}, u32[]{:S(2)}) %collective-permute-start) | collective-permute-done | bytes 524320 | tf_op jit(solution)/shard_map/ppermute | solution.py:233
  20.0 0.1 add.18
  20.1 0.0 copy-start.15
  20.1 2.2 %collective-permute-start.1 = (f32[8,128,128]{2,1,0:T(8,128)S(1)}, f32[8,128,128]{2,1,0:T(8,128)S(1)}, u32[]{:S(2)}, u32[]{:S(2)}) collective-permute-start(f32[8,128,128]{2,1,0:T(8,128)S(1)} %add.18), channel_id=1, source_target_pairs={{0,6},{2,4},{4,2},{6,0},{8,14},{10,12},{12,10},{14,8},{16,22},{18,... | collective-permute-start | bytes 1572872 | tf_op jit(solution)/shard_map/ppermute | solution.py:233
  22.3 22.5 %collective-permute-done.1.refs_1_ = f32[8,128,128]{2,1,0:T(8,128)S(1)} collective-permute-done((f32[8,128,128]{2,1,0:T(8,128)S(1)}, f32[8,128,128]{2,1,0:T(8,128)S(1)}, u32[]{:S(2)}, u32[]{:S(2)}) %collective-permute-start.1) | collective-permute-done | bytes 524320 | tf_op jit(solution)/shard_map/ppermute | solution.py:233
  44.7 0.0 copy-start.2
  44.7 0.1 add.19
  44.8 0.0 copy-start.12
  44.8 5.4 %collective-permute-start.2 = (f32[8,128,128]{2,1,0:T(8,128)S(1)}, f32[8,128,128]{2,1,0:T(8,128)S(1)}, u32[]{:S(2)}, u32[]{:S(2)}) collective-permute-start(f32[8,128,128]{2,1,0:T(8,128)S(1)} %add.19), channel_id=1, source_target_pairs={{0,14},{2,12},{4,10},{6,8},{8,6},{10,4},{12,2},{14,0},{16,30},{18,... | collective-permute-start | bytes 1572872 | tf_op jit(solution)/shard_map/ppermute | solution.py:233
  50.2 10.8 %collective-permute-done.2.refs_2_ = f32[8,128,128]{2,1,0:T(8,128)S(1)} collective-permute-done((f32[8,128,128]{2,1,0:T(8,128)S(1)}, f32[8,128,128]{2,1,0:T(8,128)S(1)}, u32[]{:S(2)}, u32[]{:S(2)}) %collective-permute-start.2) | collective-permute-done | bytes 524320 | tf_op jit(solution)/shard_map/ppermute | solution.py:233
  61.0 0.0 copy-start.4
  61.0 0.1 add.20
  61.1 1.7 %collective-permute-start.3 = (f32[8,128,128]{2,1,0:T(8,128)S(1)}, f32[8,128,128]{2,1,0:T(8,128)S(1)}, u32[]{:S(2)}, u32[]{:S(2)}) collective-permute-start(f32[8,128,128]{2,1,0:T(8,128)S(1)} %add.20), channel_id=1, source_target_pairs={{0,16},{2,18},{4,20},{6,22},{8,24},{10,26},{12,28},{14,30},{16,0},... | collective-permute-start | bytes 1572872 | tf_op jit(solution)/shard_map/ppermute | solution.py:233
  62.8 10.1 %collective-permute-done.3.refs_0_ = f32[8,128,128]{2,1,0:T(8,128)S(1)} collective-permute-done((f32[8,128,128]{2,1,0:T(8,128)S(1)}, f32[8,128,128]{2,1,0:T(8,128)S(1)}, u32[]{:S(2)}, u32[]{:S(2)}) %collective-permute-start.3) | collective-permute-done | bytes 524320 | tf_op jit(solution)/shard_map/ppermute | solution.py:233
  72.9 0.0 copy-start.6
  72.9 0.1 add.21
  73.0 0.0 copy-done.2
  73.0 3.1 %collective-permute-start.4 = (f32[8,128,128]{2,1,0:T(8,128)S(1)}, f32[8,128,128]{2,1,0:T(8,128)S(1)}, u32[]{:S(2)}, u32[]{:S(2)}) collective-permute-start(f32[8,128,128]{2,1,0:T(8,128)S(1)} %add.21), channel_id=1, source_target_pairs={{0,48},{2,50},{4,52},{6,54},{8,56},{10,58},{12,60},{14,62},{16,32}... | collective-permute-start | bytes 1572872 | tf_op jit(solution)/shard_map/ppermute | solution.py:233
  76.2 0.0 copy-done.15
  76.2 0.4 copy.9.codes_ref
  76.5 0.0 copy-done.4
  76.5 0.0 copy-done.6
  76.5 0.0 copy-done.12
  76.5 0.0 copy-start.14
  76.6 1.1 split_heads.1.q_ref
  77.7 7.6 %collective-permute-done.4.refs_1_ = f32[8,128,128]{2,1,0:T(8,128)S(1)} collective-permute-done((f32[8,128,128]{2,1,0:T(8,128)S(1)}, f32[8,128,128]{2,1,0:T(8,128)S(1)}, u32[]{:S(2)}, u32[]{:S(2)}) %collective-permute-start.4) | collective-permute-done | bytes 524320 | tf_op jit(solution)/shard_map/ppermute | solution.py:233
  85.2 0.0 copy-start.8
  85.3 0.9 add.22
  86.2 1.5 %collective-permute-start.5 = (f32[8,128,128]{2,1,0:T(8,128)}, f32[8,128,128]{2,1,0:T(8,128)}, u32[]{:S(2)}, u32[]{:S(2)}) collective-permute-start(f32[8,128,128]{2,1,0:T(8,128)} %add.22), channel_id=1, source_target_pairs={{0,64},{2,66},{4,68},{6,70},{8,72},{10,74},{12,76},{14,78},{16,80}... | collective-permute-start | bytes 1572872 | tf_op jit(solution)/shard_map/ppermute | solution.py:233
  87.6 0.0 copy-done.8
  87.6 0.0 copy-done.14
  87.6 10.2 %local_part.1.total_ref = f32[8,128,1024]{2,1,0:T(8,128)S(1)} custom-call(bf16[8,1024,128]{2,1,0:T(8,128)(2,1)S(1)} %split_heads.1.q_ref, bf16[8,1024,128]{2,1,0:T(8,128)(2,1)S(1)} %get-tuple-element.8.k_ref, bf16[8,128,1024]{2,1,0:T(8,128)(2,1)S(1)} %get-tuple-element.9.v_ref, s32[8,18,1024]{2,1,0:T(8,128)S(1)} %copy.9.codes_ref, s32[128,128]{1,0:T(8,128)S(1)} %copy-done.14), custom_call_target="tpu_custom_call" | custom-call | flops 17179869184 | bytes 16777216 | tf_op jit(solution)/shard_map/local_part/pallas_call | solution.py:136
  97.9 0.0 copy-start
  97.9 1.9 %copy-done = f32[8,128,1024]{2,1,0:T(8,128)} copy-done((f32[8,128,1024]{2,1,0:T(8,128)}, f32[8,128,1024]{2,1,0:T(8,128)S(1)}, u32[]{:S(2)}) %copy-start) | copy-done | bytes 4194328
  99.8 0.0 collective-permute-done.5.refs_2_
  99.8 1.3 %add.23 = f32[8,128,128]{2,1,0:T(8,128)S(1)} add(f32[8,128,128]{2,1,0:T(8,128)} %add.22, f32[8,128,128]{2,1,0:T(8,128)} %collective-permute-done.5.refs_2_) | non-fusion elementwise | flops 131072 | bytes 1572864 | tf_op jit(solution)/shard_map/add | solution.py:250
  101.1 2.2 %collective-permute-start.6 = (f32[8,128,128]{2,1,0:T(8,128)S(1)}, f32[8,128,128]{2,1,0:T(8,128)S(1)}, u32[]{:S(2)}, u32[]{:S(2)}) collective-permute-start(f32[8,128,128]{2,1,0:T(8,128)S(1)} %add.23), channel_id=1, source_target_pairs={{0,192},{2,194},{4,196},{6,198},{8,200},{10,202},{12,204},{14,206}... | collective-permute-start | bytes 1572872 | tf_op jit(solution)/shard_map/ppermute | solution.py:233
  103.3 0.0 copy-start.1
  103.3 2.2 %copy-done.1 = f32[8,128,1024]{2,1,0:T(8,128)S(1)} copy-done((f32[8,128,1024]{2,1,0:T(8,128)S(1)}, f32[8,128,1024]{2,1,0:T(8,128)}, u32[]{:S(2)}) %copy-start.1) | copy-done | bytes 4194328
  105.5 0.0 copy-start.3
  105.5 1.0 copy-done.3
  106.5 0.0 copy-start.5
  106.5 1.0 copy-done.5
  107.6 0.0 copy-start.7
  107.6 0.0 copy-start.9
  107.6 5.3 %add_cross.2.total_ref = f32[8,128,1024]{2,1,0:T(8,128)S(1)} custom-call(f32[8,128,1024]{2,1,0:T(8,128)S(1)} %copy-done.1, bf16[8,1024,128]{2,1,0:T(8,128)(2,1)S(1)} %split_heads.1.q_ref, s32[8,18,1024]{2,1,0:T(8,128)S(1)} %copy.9.codes_ref, f32[7]{0:T(128)S(1)} %convert_multiply_fusion.flag_ref, ...), custom_call_target="tpu_custom_call", output_to_operand_aliasing={{}: (0, {})} | custom-call | flops 3221225472 | bytes 12582912 | tf_op jit(solution)/shard_map/add_cross/pallas_call | solution.py:176
  112.8 0.0 copy-done.7
  112.9 0.0 copy-done.9
  112.9 0.0 copy-start.13
  112.9 6.4 %add_cross.3.total_ref = f32[8,128,1024]{2,1,0:T(8,128)S(1)} custom-call(f32[8,128,1024]{2,1,0:T(8,128)S(1)} %add_cross.2.total_ref, bf16[8,1024,128]{2,1,0:T(8,128)(2,1)S(1)} %split_heads.1.q_ref, s32[8,18,1024]{2,1,0:T(8,128)S(1)} %copy.9.codes_ref, f32[7]{0:T(128)S(1)} %convert_multiply_fusion.flag_ref, ...), custom_call_target="tpu_custom_call", output_to_operand_aliasing={{}: (0, {})} | custom-call | flops 3221225472 | bytes 12582912 | tf_op jit(solution)/shard_map/add_cross/pallas_call | solution.py:176
  119.3 0.0 collective-permute-done.6.refs_0_
  119.3 0.0 copy-done.13
  119.3 4.6 %finish.1 = bf16[8192,128]{1,0:T(8,128)(2,1)} custom-call(f32[8,128,1024]{2,1,0:T(8,128)S(1)} %add_cross.3.total_ref, bf16[8,1024,128]{2,1,0:T(8,128)(2,1)S(1)} %split_heads.1.q_ref, s32[8,18,1024]{2,1,0:T(8,128)S(1)} %copy.9.codes_ref, f32[7]{0:T(128)S(1)} %convert_multiply_fusion.flag_ref, f32[8,128]{1,0:T(8,128)S(1)} %copy-done.13, ...), custom_call_target="tpu_custom_call" | custom-call | flops 1073741824 | bytes 10485760 | tf_op jit(solution)/shard_map/finish/pallas_call | solution.py:211
  (1 shorter events, 0.0 us)
Async XLA Ops:
  0.0 1.6 %copy-start.10 = (bf16[1024,8,128]{2,1,0:T(8,128)(2,1)S(1)}, bf16[1024,8,128]{2,1,0:T(8,128)(2,1)}, u32[]{:S(2)}) copy-start(bf16[1024,8,128]{2,1,0:T(8,128)(2,1)} %param.7) | copy-start | bytes 6291460
  1.6 1.6 %copy-start.11 = (bf16[1024,8,128]{2,1,0:T(8,128)(2,1)S(1)}, bf16[1024,8,128]{2,1,0:T(8,128)(2,1)}, u32[]{:S(2)}) copy-start(bf16[1024,8,128]{2,1,0:T(8,128)(2,1)} %param.8) | copy-start | bytes 6291460
  6.3 13.8 %collective-permute-start = (f32[8,128,128]{2,1,0:T(8,128)S(1)}, f32[8,128,128]{2,1,0:T(8,128)S(1)}, u32[]{:S(2)}, u32[]{:S(2)}) collective-permute-start(f32[8,128,128]{2,1,0:T(8,128)S(1)} %get-tuple-element.10), channel_id=1, source_target_pairs={{0,2},{2,0},{4,6},{6,4},{8,10},{10,8},{12,14},{14,12},{16,18},{18,... | collective-permute-start | bytes 1572872 | tf_op jit(solution)/shard_map/ppermute | solution.py:233
  20.1 56.1 %copy-start.15 = (s32[8,18,1024]{2,0,1:T(8,128)S(1)}, s32[8,18,1024]{2,0,1:T(8,128)}, u32[]{:S(2)}) copy-start(s32[8,18,1024]{2,0,1:T(8,128)} %param.9) | copy-start | bytes 1769476
  20.1 24.7 %collective-permute-start.1 = (f32[8,128,128]{2,1,0:T(8,128)S(1)}, f32[8,128,128]{2,1,0:T(8,128)S(1)}, u32[]{:S(2)}, u32[]{:S(2)}) collective-permute-start(f32[8,128,128]{2,1,0:T(8,128)S(1)} %add.18), channel_id=1, source_target_pairs={{0,6},{2,4},{4,2},{6,0},{8,14},{10,12},{12,10},{14,8},{16,22},{18,... | collective-permute-start | bytes 1572872 | tf_op jit(solution)/shard_map/ppermute | solution.py:233
  44.7 28.3 %copy-start.2 = (f32[8,128,128]{2,1,0:T(8,128)}, f32[8,128,128]{2,1,0:T(8,128)S(1)}, u32[]{:S(2)}) copy-start(f32[8,128,128]{2,1,0:T(8,128)S(1)} %collective-permute-done.1.refs_1_) | copy-start | bytes 1572868
  44.8 31.7 %copy-start.12 = (bf16[1024,8,128]{2,1,0:T(8,128)(2,1)S(1)}, bf16[1024,8,128]{2,1,0:T(8,128)(2,1)}, u32[]{:S(2)}) copy-start(bf16[1024,8,128]{2,1,0:T(8,128)(2,1)} %param.6) | copy-start | bytes 6291460
  44.8 16.1 %collective-permute-start.2 = (f32[8,128,128]{2,1,0:T(8,128)S(1)}, f32[8,128,128]{2,1,0:T(8,128)S(1)}, u32[]{:S(2)}, u32[]{:S(2)}) collective-permute-start(f32[8,128,128]{2,1,0:T(8,128)S(1)} %add.19), channel_id=1, source_target_pairs={{0,14},{2,12},{4,10},{6,8},{8,6},{10,4},{12,2},{14,0},{16,30},{18,... | collective-permute-start | bytes 1572872 | tf_op jit(solution)/shard_map/ppermute | solution.py:233
  61.0 15.5 %copy-start.4 = (f32[8,128,128]{2,1,0:T(8,128)}, f32[8,128,128]{2,1,0:T(8,128)S(1)}, u32[]{:S(2)}) copy-start(f32[8,128,128]{2,1,0:T(8,128)S(1)} %collective-permute-done.2.refs_2_) | copy-start | bytes 1572868
  61.1 11.8 %collective-permute-start.3 = (f32[8,128,128]{2,1,0:T(8,128)S(1)}, f32[8,128,128]{2,1,0:T(8,128)S(1)}, u32[]{:S(2)}, u32[]{:S(2)}) collective-permute-start(f32[8,128,128]{2,1,0:T(8,128)S(1)} %add.20), channel_id=1, source_target_pairs={{0,16},{2,18},{4,20},{6,22},{8,24},{10,26},{12,28},{14,30},{16,0},... | collective-permute-start | bytes 1572872 | tf_op jit(solution)/shard_map/ppermute | solution.py:233
  72.9 3.6 %copy-start.6 = (f32[8,128,128]{2,1,0:T(8,128)}, f32[8,128,128]{2,1,0:T(8,128)S(1)}, u32[]{:S(2)}) copy-start(f32[8,128,128]{2,1,0:T(8,128)S(1)} %collective-permute-done.3.refs_0_) | copy-start | bytes 1572868
  73.0 12.2 %collective-permute-start.4 = (f32[8,128,128]{2,1,0:T(8,128)S(1)}, f32[8,128,128]{2,1,0:T(8,128)S(1)}, u32[]{:S(2)}, u32[]{:S(2)}) collective-permute-start(f32[8,128,128]{2,1,0:T(8,128)S(1)} %add.21), channel_id=1, source_target_pairs={{0,48},{2,50},{4,52},{6,54},{8,56},{10,58},{12,60},{14,62},{16,32}... | collective-permute-start | bytes 1572872 | tf_op jit(solution)/shard_map/ppermute | solution.py:233
  76.5 11.1 %copy-start.14 = (s32[128,128]{1,0:T(8,128)S(1)}, s32[128,128]{1,0:T(8,128)}, u32[]{:S(2)}) copy-start(s32[128,128]{1,0:T(8,128)} %constant.12.clone.map_ref) | copy-start | bytes 196612
  85.2 2.4 %copy-start.8 = (f32[8,128,128]{2,1,0:T(8,128)}, f32[8,128,128]{2,1,0:T(8,128)S(1)}, u32[]{:S(2)}) copy-start(f32[8,128,128]{2,1,0:T(8,128)S(1)} %collective-permute-done.4.refs_1_) | copy-start | bytes 1572868
  86.2 13.6 %collective-permute-start.5 = (f32[8,128,128]{2,1,0:T(8,128)}, f32[8,128,128]{2,1,0:T(8,128)}, u32[]{:S(2)}, u32[]{:S(2)}) collective-permute-start(f32[8,128,128]{2,1,0:T(8,128)} %add.22), channel_id=1, source_target_pairs={{0,64},{2,66},{4,68},{6,70},{8,72},{10,74},{12,76},{14,78},{16,80}... | collective-permute-start | bytes 1572872 | tf_op jit(solution)/shard_map/ppermute | solution.py:233
  97.9 1.9 %copy-start = (f32[8,128,1024]{2,1,0:T(8,128)}, f32[8,128,1024]{2,1,0:T(8,128)S(1)}, u32[]{:S(2)}) copy-start(f32[8,128,1024]{2,1,0:T(8,128)S(1)} %local_part.1.total_ref) | copy-start | bytes 12582916
  101.1 18.2 %collective-permute-start.6 = (f32[8,128,128]{2,1,0:T(8,128)S(1)}, f32[8,128,128]{2,1,0:T(8,128)S(1)}, u32[]{:S(2)}, u32[]{:S(2)}) collective-permute-start(f32[8,128,128]{2,1,0:T(8,128)S(1)} %add.23), channel_id=1, source_target_pairs={{0,192},{2,194},{4,196},{6,198},{8,200},{10,202},{12,204},{14,206}... | collective-permute-start | bytes 1572872 | tf_op jit(solution)/shard_map/ppermute | solution.py:233
  103.3 2.2 %copy-start.1 = (f32[8,128,1024]{2,1,0:T(8,128)S(1)}, f32[8,128,1024]{2,1,0:T(8,128)}, u32[]{:S(2)}) copy-start(f32[8,128,1024]{2,1,0:T(8,128)} %copy-done) | copy-start | bytes 12582916
  105.5 1.0 copy-start.3
  106.5 1.0 copy-start.5
  107.6 5.3 %copy-start.7 = (f32[8,128,128]{2,1,0:T(8,128)S(1)}, f32[8,128,128]{2,1,0:T(8,128)}, u32[]{:S(2)}) copy-start(f32[8,128,128]{2,1,0:T(8,128)} %copy-done.6) | copy-start | bytes 1572868
  107.6 5.3 %copy-start.9 = (f32[8,128,128]{2,1,0:T(8,128)S(1)}, f32[8,128,128]{2,1,0:T(8,128)}, u32[]{:S(2)}) copy-start(f32[8,128,128]{2,1,0:T(8,128)} %copy-done.8) | copy-start | bytes 1572868
  112.9 6.4 %copy-start.13 = (f32[8,128]{1,0:T(8,128)S(1)}, f32[8,128]{1,0:T(8,128)}, u32[]{:S(2)}) copy-start(f32[8,128]{1,0:T(8,128)} %gain_ref.1) | copy-start | bytes 12292

commit v2 on v0

v2 whole, which is shorter than its diff:
```python
import functools

import jax
import jax.numpy as jnp
import numpy as np
from jax import lax
from jax.experimental import pallas as pl
from jax.experimental.pallas import tpu as pltpu
from jax.sharding import PartitionSpec as P

STATES_MIB = 58
NT = (((1,), (1,)), ((), ()))
VMEM = pl.BlockSpec(memory_space=pltpu.VMEM)
SMEM = pl.BlockSpec(memory_space=pltpu.SMEM)
ANY = pl.BlockSpec(memory_space=pl.ANY)


def params(mib):
    return pltpu.CompilerParams(vmem_limit_bytes=mib * 1024 * 1024)


def cost(flops, nbytes):
    return pl.CostEstimate(flops=flops, bytes_accessed=nbytes, transcendentals=0)


def level_map(size):
    source = np.arange(size)[:, None]
    target = np.arange(size)[None, :]
    levels = np.zeros((size, size), np.int32)
    for shift in range(24):
        levels += (target >> shift != source >> shift).astype(np.int32)
    return np.where(source <= target, levels, -1).astype(np.int32)


def first_head(owner_ref, own_heads, half):
    return (owner_ref[0] if own_heads else 1 - owner_ref[0]) * half


def states_kernel(heads, rows, owner_ref, k_hbm, v_hbm, own_out, other_out, k_in, v_in, k_wide, v_wide, state, sems):
    chunks = k_in.shape[0]
    half = heads // 2

    def load(hbm, buffer, which, i):
        part = pl.ds(i * rows * heads, rows * heads)
        return pltpu.make_async_copy(hbm.at[part], buffer.at[i], sems.at[which, i])

    for i in range(chunks):
        load(k_hbm, k_in, 0, i).start()
        load(v_hbm, v_in, 1, i).start()
    for i in range(chunks):
        load(k_hbm, k_in, 0, i).wait()
        load(v_hbm, v_in, 1, i).wait()
        k_wide[...] = k_in[i].astype(jnp.float32)
        v_wide[...] = v_in[i].astype(jnp.float32)
        for h in range(heads):
            key = k_wide[pl.ds(h, rows, stride=heads), :].astype(jnp.bfloat16)
            value = v_wide[pl.ds(h, rows, stride=heads), :].T.astype(jnp.bfloat16)
            product = jnp.dot(value, key, preferred_element_type=jnp.float32)
            if i:
                product = state[h] + product
            state[h] = product
    owner = owner_ref[0]
    own_out[...] = state[pl.ds(owner * half, half)]
    other_out[...] = state[pl.ds((1 - owner) * half, half)]


def make_states(key_rows, value_rows, owner, rows=128):
    length, heads, dim = key_rows.shape
    chunks = length // rows
    part = jax.ShapeDtypeStruct((heads // 2, dim, dim), jnp.float32)
    return pl.pallas_call(
        functools.partial(states_kernel, heads, rows),
        in_specs=[SMEM, ANY, ANY],
        out_specs=[VMEM, VMEM],
        out_shape=[part, part],
        scratch_shapes=[pltpu.VMEM((chunks, rows * heads, dim), jnp.bfloat16)] * 2
        + [pltpu.VMEM((rows * heads, dim), jnp.float32)] * 2
        + [pltpu.VMEM((heads, dim, dim), jnp.float32)]
        + [pltpu.SemaphoreType.DMA((2, chunks))],
        compiler_params=params(STATES_MIB),
        cost_estimate=cost(2 * heads * length * dim * dim, 4 * length * heads * dim),
        name="states",
    )(owner, key_rows.reshape(length * heads, dim), value_rows.reshape(length * heads, dim))


def split_kernel(heads, rows, _, q_ref, k_ref, v_ref, q_out, k_out, v_out, q_wide, k_wide, v_wide):
    for i in range(q_out.shape[1] // rows):
        span = slice(i * rows, (i + 1) * rows)
        flat = slice(i * rows * heads, (i + 1) * rows * heads)
        q_wide[...] = q_ref[flat, :].astype(jnp.float32)
        k_wide[...] = k_ref[flat, :].astype(jnp.float32)
        v_wide[...] = v_ref[flat, :].astype(jnp.float32)
        for h in range(heads):
            q_out[h, span, :] = q_wide[pl.ds(h, rows, stride=heads), :].astype(jnp.bfloat16)
            k_out[h, span, :] = k_wide[pl.ds(h, rows, stride=heads), :].astype(jnp.bfloat16)
            v_out[h, :, span] = v_wide[pl.ds(h, rows, stride=heads), :].T.astype(jnp.bfloat16)


def split_heads(earlier, query_rows, key_rows, value_rows, rows=256):
    length, heads, dim = query_rows.shape
    straight = jax.ShapeDtypeStruct((heads, length, dim), jnp.bfloat16)
    turned = jax.ShapeDtypeStruct((heads, dim, length), jnp.bfloat16)
    return pl.pallas_call(
        functools.partial(split_kernel, heads, rows),
        in_specs=[ANY] + [VMEM] * 3,
        out_specs=[VMEM] * 3,
        out_shape=[straight, straight, turned],
        scratch_shapes=[pltpu.VMEM((rows * heads, dim), jnp.float32)] * 3,
        compiler_params=params(12),
        cost_estimate=cost(0, 12 * length * heads * dim),
        name="split_heads",
    )(earlier, *[each.reshape(length * heads, dim) for each in (query_rows, key_rows, value_rows)])


def local_kernel(length, tile, small, own_heads, owner_ref, q_ref, k_ref, v_ref, codes_ref, map_ref, *refs):
    out_ref = refs[-1]
    low_levels = small.bit_length()

    half = q_ref.shape[0] // 2
    begin = first_head(owner_ref, own_heads, half)

    @pl.loop(0, half)
    def _(i):
        h = begin + i
        weights = [codes_ref[level, pl.ds(h, 1), :].astype(jnp.float32) * (1.0 / 64.0) for level in range(length.bit_length())]
        levels = map_ref[...]
        masks = [levels == level for level in range(low_levels)]
        for t in range(length // tile):
            columns = slice(t * tile, (t + 1) * tile)
            count = (t + 1) * tile
            scores = lax.dot_general(
                k_ref[h, :count, :], q_ref[h, columns, :], NT, preferred_element_type=jnp.float32
            )
            pieces = []
            for s in range(t):
                level = (t ^ s).bit_length() + tile.bit_length() - 1
                piece = scores[s * tile:(s + 1) * tile] * weights[level][:, columns]
                pieces.append(piece.astype(jnp.bfloat16))
            for i in range(tile // small):
                row = []
                for j in range(tile // small):
                    first = t * tile + j * small
                    lanes = slice(first, first + small)
                    part = scores[t * tile + i * small:t * tile + (i + 1) * small, j * small:(j + 1) * small]
                    if j < i:
                        row.append(jnp.zeros((small, small), jnp.bfloat16))
                        continue
                    if j > i:
                        level = (i ^ j).bit_length() + small.bit_length() - 1
                        picked = weights[level][:, lanes]
                    else:
                        picked = jnp.zeros((small, small), jnp.float32)
                        for level in range(low_levels):
                            picked = jnp.where(masks[level], weights[level][:, lanes], picked)
                    row.append((part * picked).astype(jnp.bfloat16))
                pieces.append(jnp.concatenate(row, axis=1))
            weighted = jnp.concatenate(pieces, axis=0) if len(pieces) > 1 else pieces[0]
            out_ref[h, :, columns] = jnp.dot(
                v_ref[h, :, :count], weighted, preferred_element_type=jnp.float32
            )


def local_part(total, query, key, value, codes, owner, own_heads, tile=256, small=128):
    every, length, dim = query.shape
    operands = [owner, query, key, value, codes, jnp.asarray(level_map(small))]
    specs = [SMEM] + [VMEM] * (len(operands) - 1)
    aliases = {}
    if total is not None:
        aliases = {len(operands): 0}
        operands.append(total)
        specs.append(VMEM)
    return pl.pallas_call(
        functools.partial(local_kernel, length, tile, small, own_heads),
        in_specs=specs,
        out_specs=VMEM,
        out_shape=jax.ShapeDtypeStruct((every, dim, length), jnp.float32),
        input_output_aliases=aliases,
        compiler_params=params(12),
        cost_estimate=cost(5 * every * length * length * dim, 8 * length * every * dim),
        name="local_part",
    )(*operands)


def bucket_products(buckets, query):
    stacked = jnp.concatenate(buckets, axis=0) if len(buckets) > 1 else buckets[0]
    high = stacked.astype(jnp.bfloat16)
    low = (stacked - high.astype(jnp.float32)).astype(jnp.bfloat16)
    products = lax.dot_general(
        jnp.concatenate([high, low], axis=1),
        jnp.concatenate([query, query], axis=1),
        NT,
        preferred_element_type=jnp.float32,
    )
    dim = query.shape[1]
    return [products[i * dim:(i + 1) * dim] for i in range(len(buckets))]


def cross_kernel(bits, first, own_heads, owner_ref, flag_ref, total_ref, q_ref, codes_ref, *refs):
    out_ref = refs[-1]
    half = q_ref.shape[0] // 2
    begin = first_head(owner_ref, own_heads, half)

    @pl.loop(0, half)
    def _(i):
        h = begin + i
        total = total_ref[h]
        products = bucket_products([ref[i] for ref in refs[:-1]], q_ref[h])
        for product, bit in zip(products, bits):
            scale = codes_ref[first + bit, pl.ds(h, 1), :].astype(jnp.float32) * flag_ref[bit]
            total = total + scale * product
        out_ref[h] = total


def add_cross(total, query, codes, flags, owner, own_heads, buckets, bits, first):
    heads, length, dim = query.shape
    return pl.pallas_call(
        functools.partial(cross_kernel, bits, first, own_heads),
        in_specs=[SMEM, SMEM] + [VMEM] * (3 + len(bits)),
        out_specs=VMEM,
        out_shape=jax.ShapeDtypeStruct((heads, dim, length), jnp.float32),
        input_output_aliases={2: 0},
        compiler_params=params(12),
        cost_estimate=cost(3 * len(bits) * heads * length * dim * dim, 3 * length * heads * dim),
        name="add_cross",
    )(owner, flags, total, query, codes, *buckets)


def finish_kernel(bits, first, rows, own_heads, owner_ref, flag_ref, total_ref, q_ref, codes_ref, gain_ref, *refs):
    buckets = refs[:len(bits)]
    if own_heads:
        wide = refs[-1]
    else:
        wide, out_hbm, narrow, sems = refs[-4:]
    heads, dim, length = total_ref.shape
    half = heads // 2
    chunks = length // rows
    begin = first_head(owner_ref, own_heads, half)

    def store(i):
        part = pl.ds(i * rows * heads, rows * heads)
        return pltpu.make_async_copy(narrow.at[i], out_hbm.at[part], sems.at[i])

    for c in range(chunks):
        columns = slice(c * rows, (c + 1) * rows)
        for i in range(half):
            h = begin + i
            total = total_ref[h, :, columns]
            products = bucket_products([ref[i] for ref in buckets], q_ref[h, columns, :])
            for product, bit in zip(products, bits):
                scale = codes_ref[first + bit, pl.ds(h, 1), columns].astype(jnp.float32) * flag_ref[bit]
                total = total + scale * product
            mean_square = jnp.sum(total * total, axis=0, keepdims=True) * (1.0 / dim)
            normed = total * lax.rsqrt(mean_square + 1e-06)
            wide[pl.ds(c * rows * heads + h, rows, stride=heads), :] = normed.T * gain_ref[pl.ds(h, 1), :]
        if not own_heads:
            narrow[c] = wide[c * rows * heads:(c + 1) * rows * heads, :].astype(jnp.bfloat16)
            store(c).start()
    if not own_heads:
        for c in range(chunks):
            store(c).wait()


def finish_own(total, query, codes, flags, owner, gain, buckets, bits, first, rows=256):
    heads, length, dim = query.shape
    return pl.pallas_call(
        functools.partial(finish_kernel, bits, first, rows, True),
        in_specs=[SMEM, SMEM] + [VMEM] * (4 + len(bits)),
        out_specs=VMEM,
        out_shape=jax.ShapeDtypeStruct((length * heads, dim), jnp.float32),
        compiler_params=params(12),
        cost_estimate=cost(4 * heads * length * dim * dim, 4 * length * heads * dim),
        name="finish_own",
    )(owner, flags, total, query, codes, gain, *buckets)


def finish_other(wide, total, query, codes, flags, owner, gain, buckets, bits, first, rows=256):
    heads, length, dim = query.shape
    _, out = pl.pallas_call(
        functools.partial(finish_kernel, bits, first, rows, False),
        in_specs=[SMEM, SMEM] + [VMEM] * (5 + len(bits)),
        out_specs=[VMEM, ANY],
        out_shape=[
            jax.ShapeDtypeStruct((length * heads, dim), jnp.float32),
            jax.ShapeDtypeStruct((length * heads, dim), jnp.bfloat16),
        ],
        scratch_shapes=[
            pltpu.VMEM((length // rows, rows * heads, dim), jnp.bfloat16),
            pltpu.SemaphoreType.DMA((length // rows,)),
        ],
        input_output_aliases={6 + len(bits): 0},
        compiler_params=params(12),
        cost_estimate=cost(4 * heads * length * dim * dim, 10 * length * heads * dim),
        name="finish_other",
    )(owner, flags, total, query, codes, gain, *buckets, wide)
    return out.reshape(length, heads, dim)


def swapped(block, mask):
    count = lax.axis_size("seq")
    return lax.ppermute(block, "seq", [(i, i ^ mask) for i in range(count)])


def next_along_z(block):
    count = lax.axis_size("seq")
    route = []
    for i in range(count):
        ring = i & ~7
        step = 1 if i & 1 else -1
        route.append((i, ring | (i + step) & 7))
    return lax.ppermute(block, "seq", route)


def shards(query_rows, key_rows, value_rows, level_codes, norm_gain):
    bit_count = lax.axis_size("seq").bit_length() - 1
    first = level_codes.shape[1] - bit_count
    position = lax.axis_index("seq")
    bits = jnp.arange(bit_count, dtype=jnp.int32)
    flags = (position >> bits & 1).astype(jnp.float32) * (1.0 / 64.0)
    owner = position & 1
    half_id = owner.reshape(1).astype(jnp.int32)

    codes = jnp.transpose(level_codes, (1, 0, 2))
    own_state, other_state = make_states(key_rows, value_rows, half_id)
    half = own_state.shape[0]

    own0 = swapped(other_state, 1)
    query, key, value = split_heads(own_state, query_rows, key_rows, value_rows)
    own0, own_state, query = lax.optimization_barrier((own0, own_state, query))
    block_sum = own_state + own0

    def local(total, own_heads):
        return local_part(total, query, key, value, codes, half_id, own_heads)

    def cross(total, own_heads, buckets, bits):
        return add_cross(total, query, codes, flags, half_id, own_heads, buckets, bits, first)

    other0 = swapped(own_state, 1)
    own1 = swapped(block_sum, 2)
    total = local(None, True)
    other0, own1, total = lax.optimization_barrier((other0, own1, total))
    block_sum = block_sum + own1
    own2 = swapped(block_sum, 4)
    total = local(total, False)
    total = cross(total, True, [own0, own1], (0, 1))
    own2, total = lax.optimization_barrier((own2, total))
    block_sum = block_sum + own2
    own3, left, right = [swapped(block_sum, mask) for mask in (8, 16, 24)]
    total = cross(total, True, [own2], (2,))
    own1, own2, total = lax.optimization_barrier((own1, own2, total))
    low = swapped(jnp.concatenate([own1, own2], axis=0), 1)
    own3, left, right, total = lax.optimization_barrier((own3, left, right, total))
    own4 = left + right
    block_sum = block_sum + (own3 + own4)
    own5, left, right = [swapped(block_sum, mask) for mask in (32, 64, 96)]
    total = cross(total, True, [own3, own4], (3, 4))
    own3, own4, total = lax.optimization_barrier((own3, own4, total))
    other3 = swapped(own3, 1)
    other4 = next_along_z(own4)
    total = cross(total, False, [other0, low[:half], low[half:]], (0, 1, 2))
    own5, left, right, total = lax.optimization_barrier((own5, left, right, total))
    own6 = left + right
    other5 = swapped(own5, 1)
    other6 = next_along_z(own6)
    wide = finish_own(total, query, codes, flags, half_id, norm_gain, (own5, own6), (5, 6), first)
    total, wide = lax.optimization_barrier((total, wide))
    total = cross(total, False, [other3, other4], (3, 4))
    return finish_other(
        wide, total, query, codes, flags, half_id, norm_gain, (other5, other6), (5, 6), first
    )


def solution(mesh):
    return jax.shard_map(
        shards,
        mesh=mesh,
        in_specs=(
            P("seq", "head", None),
            P("seq", "head", None),
            P("seq", "head", None),
            P("head", None, "seq"),
            P("head", None),
        ),
        out_specs=P("seq", "head", None),
        check_vma=False,
    )
```

time: 252 us -> 84.7 us (0.34)
  matrix products: 138 us -> 0 us
  waiting for transfers between devices: 80.1 us -> 11.4 us
  Pallas kernels: 0 us -> 33 us
  starting transfers between devices: 15 us -> 37.1 us
  local copies, waits for them, and re-layouts: 10.2 us -> 2.6 us
  other arithmetic: 6.48 us -> 0.22 us
    dot_general x23 -> x0, matrix products: 138 us -> none  [the longest x8 91 us: attend_scores(): return jnp.dot(weighted, value_head, preferred_element_type=jnp.float32)]
    ppermute x7 -> x15, waiting for transfers between devices: 80.1 us -> 11.4 us  [the longest x13 11.3 us: swapped(): return lax.ppermute(block, 'seq', [(i, i ^ mask) for i in range(count)])]
    pallas_call x0 -> x11, Pallas kernels: none -> 33 us  [the longest x2 10.2 us: local_part(): pl.pallas_call(functools.partial(local_kernel, length, tile, small, own_h...]
    ppermute x7 -> x15, starting transfers between devices: 15 us -> 37.1 us  [the longest x13 31.4 us: swapped(): return lax.ppermute(block, 'seq', [(i, i ^ mask) for i in range(count)])]
    convert_element_type x1 -> x0, local copies, waits for them, and re-layouts: 2.89 us -> none  [shards(): (result * lax.rsqrt(mean_square + 1e-06) * norm_gain[None]).astype(jnp.bf...]
  transfers between devices with their start and end apart: 7 -> 15, of which waited for: 7 -> 6; matrix products, arithmetic and copies ran while one was open for 10% -> 0% of each run, Pallas kernels for 0% -> 30%
where the time goes in v2:
time: 84.7 us; the launch traced here: 84.6 us
  starting transfers between devices  37.1 us (44%)
  Pallas kernels  33 us (39%)
  waiting for transfers between devices  11.4 us (13%)
  local copies, waits for them, and re-layouts  2.6 us (3%)
    ppermute x13, starting transfers between devices, swapped(): return lax.ppermute(block, 'seq', [(i, i ^ mask) for i in range(count)])  31.4 us
    ppermute x13, waiting for transfers between devices, swapped(): return lax.ppermute(block, 'seq', [(i, i ^ mask) for i in range(count)])  11.3 us
    pallas_call x2, Pallas kernels, local_part(): pl.pallas_call(functools.partial(local_kernel, length, tile, small, own_h...  10.2 us
    pallas_call x5, Pallas kernels, add_cross(): pl.pallas_call(functools.partial(cross_kernel, bits, first, own_heads), i...  9.71 us
    ppermute x2, starting transfers between devices, next_along_z(): return lax.ppermute(block, 'seq', route)  5.68 us
    pallas_call x1, Pallas kernels, make_states(): pl.pallas_call(functools.partial(states_kernel, heads, rows), in_specs=[S...  4.26 us
    pallas_call x1, Pallas kernels, finish_other(): pl.pallas_call(functools.partial(finish_kernel, bits, first, rows, False)...  3.42 us
    pallas_call x1, Pallas kernels, split_heads(): pl.pallas_call(functools.partial(split_kernel, heads, rows), in_specs=[AN...  3.36 us
  transfers between devices with their start and end apart: 15, of which 6 were waited for; matrix products, arithmetic and copies ran while one was open for 0% of the time, Pallas kernels for 30%

profile of v2, /device:TPU:30, one launch (start us, length us, event | category | flops | bytes accessed | tf_op | source)
XLA Modules:
  0.0 84.6 jit_solution(8657770358208994750)
XLA Ops:
  0.0 0.0 copy-start.1
  0.0 0.0 copy-start.2
  0.0 4.3 %states.1 = (f32[4,128,128]{2,1,0:T(8,128)}, f32[4,128,128]{2,1,0:T(8,128)}) custom-call(s32[1]{0:T(128)} %bitcast.owner_ref, bf16[8192,128]{1,0:T(8,128)(2,1)} %bitcast.15, bf16[8192,128]{1,0:T(8,128)(2,1)} %bitcast.17), custom_call_target="tpu_custom_call" | custom-call | flops 268435456 | bytes 4194304 | tf_op jit(solution)/shard_map/states/pallas_call | solution.py:71
  4.3 0.0 copy-start
  4.3 2.0 %collective-permute-start = (f32[4,128,128]{2,1,0:T(8,128)}, f32[4,128,128]{2,1,0:T(8,128)S(1)}, u32[]{:S(2)}, u32[]{:S(2)}) collective-permute-start(f32[4,128,128]{2,1,0:T(8,128)} %get-tuple-element.35), channel_id=1, source_target_pairs={{0,2},{2,0},{4,6},{6,4},{8,10},{10,8},{12,14},{14,12},{16,18},{18,... | collective-permute-start | bytes 786440 | tf_op jit(solution)/shard_map/ppermute | solution.py:300
  6.3 0.0 copy-done.1
  6.3 0.0 copy-done.2
  6.3 0.0 copy-start.3
  6.3 1.6 %copy-done.3 = bf16[1024,8,128]{2,1,0:T(8,128)(2,1)S(1)} copy-done((bf16[1024,8,128]{2,1,0:T(8,128)(2,1)S(1)}, bf16[1024,8,128]{2,1,0:T(8,128)(2,1)}, u32[]{:S(2)}) %copy-start.3) | copy-done | bytes 2097176
  7.9 0.0 copy-start.4
  7.9 0.9 %copy-done.4 = f32[4,128,128]{2,1,0:T(8,128)S(1)} copy-done((f32[4,128,128]{2,1,0:T(8,128)S(1)}, f32[4,128,128]{2,1,0:T(8,128)}, u32[]{:S(2)}) %copy-start.4) | copy-done | bytes 262168
  8.8 0.0 copy-start.6
  8.8 3.4 %split_heads.1 = (bf16[8,1024,128]{2,1,0:T(8,128)(2,1)S(1)}, bf16[8,1024,128]{2,1,0:T(8,128)(2,1)S(1)}, bf16[8,128,1024]{2,1,0:T(8,128)(2,1)S(1)}) custom-call(f32[4,128,128]{2,1,0:T(8,128)S(1)} %copy-done.4, bf16[8192,128]{1,0:T(8,128)(2,1)S(1)} %bitcast.19, bf16[8192,128]{1,0:T(8,128)(2,1)S(1)} %bitcast.16, bf16[8192,128]{1,0:T(8,128)(2,1)S(1)} %bitcast.18), custom_call_target="tpu_custom_call" | custom-call | bytes 12582912 | tf_op jit(solution)/shard_map/split_heads/pallas_call | solution.py:103
  12.2 0.6 collective-permute-done.refs_0_
  12.8 1.7 %collective-permute-start.1 = (f32[4,128,128]{2,1,0:T(8,128)S(1)}, f32[4,128,128]{2,1,0:T(8,128)S(1)}, u32[]{:S(2)}, u32[]{:S(2)}) collective-permute-start(f32[4,128,128]{2,1,0:T(8,128)S(1)} %copy-done.4), channel_id=1, source_target_pairs={{0,2},{2,0},{4,6},{6,4},{8,10},{10,8},{12,14},{14,12},{16,18},{18,... | collective-permute-start | bytes 786440 | tf_op jit(solution)/shard_map/ppermute | solution.py:300
  14.6 3.4 %collective-permute-start.2 = (f32[4,128,128]{2,1,0:T(8,128)S(1)}, f32[4,128,128]{2,1,0:T(8,128)S(1)}, u32[]{:S(2)}, u32[]{:S(2)}) collective-permute-start(f32[4,128,128]{2,1,0:T(8,128)S(1)} %add.21), channel_id=1, source_target_pairs={{0,4},{2,6},{4,0},{6,2},{8,12},{10,14},{12,8},{14,10},{16,20},{18,... | collective-permute-start | bytes 786440 | tf_op jit(solution)/shard_map/ppermute | solution.py:300
  17.9 0.0 copy-done
  17.9 0.0 copy-done.6
  17.9 5.1 %local_part.2.refs_0_ = f32[8,128,1024]{2,1,0:T(8,128)S(1)} custom-call(s32[1]{0:T(128)} %bitcast.owner_ref, bf16[8,1024,128]{2,1,0:T(8,128)(2,1)S(1)} %get-tuple-element.40.q_ref, bf16[8,1024,128]{2,1,0:T(8,128)(2,1)S(1)} %get-tuple-element.41.k_ref, bf16[8,128,1024]{2,1,0:T(8,128)(2,1)S(1)} %get-tuple-element.42.v_ref, s32[18,8,1024]{2,1,0:T(8,128)S(1)} %bitcast.6, ...), custom_call_target="tpu_custom_call" | custom-call | flops 5368709120 | bytes 8388608 | tf_op jit(solution)/shard_map/local_part/pallas_call | solution.py:172
  23.1 5.7 %collective-permute-done.2.refs_1_ = f32[4,128,128]{2,1,0:T(8,128)S(1)} collective-permute-done((f32[4,128,128]{2,1,0:T(8,128)S(1)}, f32[4,128,128]{2,1,0:T(8,128)S(1)}, u32[]{:S(2)}, u32[]{:S(2)}) %collective-permute-start.2) | collective-permute-done | bytes 262176 | tf_op jit(solution)/shard_map/ppermute | solution.py:300
  28.7 0.0 collective-permute-done.1.refs_0_
  28.8 5.8 %collective-permute-start.3 = (f32[4,128,128]{2,1,0:T(8,128)S(1)}, f32[4,128,128]{2,1,0:T(8,128)S(1)}, u32[]{:S(2)}, u32[]{:S(2)}) collective-permute-start(f32[4,128,128]{2,1,0:T(8,128)S(1)} %add.22), channel_id=1, source_target_pairs={{0,8},{2,10},{4,12},{6,14},{8,0},{10,2},{12,4},{14,6},{16,24},{18,... | collective-permute-start | bytes 786440 | tf_op jit(solution)/shard_map/ppermute | solution.py:300
  34.6 5.1 %local_part.3.total_ref = f32[8,128,1024]{2,1,0:T(8,128)S(1)} custom-call(s32[1]{0:T(128)} %bitcast.owner_ref, bf16[8,1024,128]{2,1,0:T(8,128)(2,1)S(1)} %get-tuple-element.40.q_ref, bf16[8,1024,128]{2,1,0:T(8,128)(2,1)S(1)} %get-tuple-element.41.k_ref, bf16[8,128,1024]{2,1,0:T(8,128)(2,1)S(1)} %get-tuple-element.42.v_ref, ...), custom_call_target="tpu_custom_call", output_to_operand_aliasing={{}: (6, {})} | custom-call | flops 5368709120 | bytes 8388608 | tf_op jit(solution)/shard_map/local_part/pallas_call | solution.py:172
  39.7 1.9 %add_cross.5.total_ref = f32[8,128,1024]{2,1,0:T(8,128)S(1)} custom-call(s32[1]{0:T(128)} %bitcast.owner_ref, f32[7]{0:T(128)S(1)} %convert_multiply_fusion.flag_ref, f32[8,128,1024]{2,1,0:T(8,128)S(1)} %local_part.3.total_ref, bf16[8,1024,128]{2,1,0:T(8,128)(2,1)S(1)} %get-tuple-element.40.q_ref, ...), custom_call_target="tpu_custom_call", output_to_operand_aliasing={{}: (2, {})} | custom-call | flops 805306368 | bytes 3145728 | tf_op jit(solution)/shard_map/add_cross/pallas_call | solution.py:216
  41.6 0.7 collective-permute-done.3.refs_0_
  42.4 0.2 collective-permute-start.6
  42.6 2.7 %collective-permute-start.5 = (f32[4,128,128]{2,1,0:T(8,128)S(1)}, f32[4,128,128]{2,1,0:T(8,128)S(1)}, u32[]{:S(2)}, u32[]{:S(2)}) collective-permute-start(f32[4,128,128]{2,1,0:T(8,128)S(1)} %add.23), channel_id=1, source_target_pairs={{0,32},{2,34},{4,36},{6,38},{8,40},{10,42},{12,44},{14,46},{16,48}... | collective-permute-start | bytes 786440 | tf_op jit(solution)/shard_map/ppermute | solution.py:300
  45.3 1.3 %collective-permute-start.4 = (f32[4,128,128]{2,1,0:T(8,128)S(1)}, f32[4,128,128]{2,1,0:T(8,128)S(1)}, u32[]{:S(2)}, u32[]{:S(2)}) collective-permute-start(f32[4,128,128]{2,1,0:T(8,128)S(1)} %add.23), channel_id=1, source_target_pairs={{0,16},{2,18},{4,20},{6,22},{8,24},{10,26},{12,28},{14,30},{16,0},... | collective-permute-start | bytes 786440 | tf_op jit(solution)/shard_map/ppermute | solution.py:300
  46.5 1.8 %add_cross.6.total_ref = f32[8,128,1024]{2,1,0:T(8,128)S(1)} custom-call(s32[1]{0:T(128)} %bitcast.owner_ref, f32[7]{0:T(128)S(1)} %convert_multiply_fusion.flag_ref, f32[8,128,1024]{2,1,0:T(8,128)S(1)} %add_cross.5.total_ref, bf16[8,1024,128]{2,1,0:T(8,128)(2,1)S(1)} %get-tuple-element.40.q_ref, ...), custom_call_target="tpu_custom_call", output_to_operand_aliasing={{}: (2, {})} | custom-call | flops 402653184 | bytes 3145728 | tf_op jit(solution)/shard_map/add_cross/pallas_call | solution.py:216
  48.4 2.1 %collective-permute-start.10 = (f32[8,128,128]{2,1,0:T(8,128)S(1)}, f32[8,128,128]{2,1,0:T(8,128)S(1)}, u32[]{:S(2)}, u32[]{:S(2)}) collective-permute-start(f32[8,128,128]{2,1,0:T(8,128)S(1)} %pad_maximum_fusion), channel_id=1, source_target_pairs={{0,2},{2,0},{4,6},{6,4},{8,10},{10,8},{12,14},{14,12},{16,18},{18,... | collective-permute-start | bytes 1572872 | tf_op jit(solution)/shard_map/ppermute | solution.py:300
  50.5 2.3 %collective-permute-done.6 = f32[4,128,128]{2,1,0:T(8,128)S(1)} collective-permute-done((f32[4,128,128]{2,1,0:T(8,128)S(1)}, f32[4,128,128]{2,1,0:T(8,128)S(1)}, u32[]{:S(2)}, u32[]{:S(2)}) %collective-permute-start.6) | collective-permute-done | bytes 262176 | tf_op jit(solution)/shard_map/ppermute | solution.py:300
  52.8 0.0 collective-permute-done.5
  52.8 0.9 %collective-permute-done.4.refs_0_ = f32[4,128,128]{2,1,0:T(8,128)S(1)} collective-permute-done((f32[4,128,128]{2,1,0:T(8,128)S(1)}, f32[4,128,128]{2,1,0:T(8,128)S(1)}, u32[]{:S(2)}, u32[]{:S(2)}) %collective-permute-start.4) | collective-permute-done | bytes 262176 | tf_op jit(solution)/shard_map/ppermute | solution.py:300
  53.7 0.1 add_add_fusion
  53.8 0.6 collective-permute-start.9
  54.4 2.5 %collective-permute-start.8 = (f32[4,128,128]{2,1,0:T(8,128)S(1)}, f32[4,128,128]{2,1,0:T(8,128)S(1)}, u32[]{:S(2)}, u32[]{:S(2)}) collective-permute-start(f32[4,128,128]{2,1,0:T(8,128)S(1)} %get-tuple-element.65), channel_id=1, source_target_pairs={{0,128},{2,130},{4,132},{6,134},{8,136},{10,138},{12,140},{14,142}... | collective-permute-start | bytes 786440 | tf_op jit(solution)/shard_map/ppermute | solution.py:300
  56.8 1.1 %collective-permute-start.7 = (f32[4,128,128]{2,1,0:T(8,128)S(1)}, f32[4,128,128]{2,1,0:T(8,128)S(1)}, u32[]{:S(2)}, u32[]{:S(2)}) collective-permute-start(f32[4,128,128]{2,1,0:T(8,128)S(1)} %get-tuple-element.65), channel_id=1, source_target_pairs={{0,64},{2,66},{4,68},{6,70},{8,72},{10,74},{12,76},{14,78},{16,80}... | collective-permute-start | bytes 786440 | tf_op jit(solution)/shard_map/ppermute | solution.py:300
  57.9 1.9 %add_cross.7.total_ref = f32[8,128,1024]{2,1,0:T(8,128)S(1)} custom-call(s32[1]{0:T(128)} %bitcast.owner_ref, f32[7]{0:T(128)S(1)} %convert_multiply_fusion.flag_ref, f32[8,128,1024]{2,1,0:T(8,128)S(1)} %add_cross.6.total_ref, bf16[8,1024,128]{2,1,0:T(8,128)(2,1)S(1)} %get-tuple-element.40.q_ref, ...), custom_call_target="tpu_custom_call", output_to_operand_aliasing={{}: (2, {})} | custom-call | flops 805306368 | bytes 3145728 | tf_op jit(solution)/shard_map/add_cross/pallas_call | solution.py:216
  59.8 3.1 %collective-permute-start.11 = (f32[4,128,128]{2,1,0:T(8,128)S(1)}, f32[4,128,128]{2,1,0:T(8,128)S(1)}, u32[]{:S(2)}, u32[]{:S(2)}) collective-permute-start(f32[4,128,128]{2,1,0:T(8,128)S(1)} %collective-permute-done.4.refs_0_), channel_id=1, source_target_pairs={{0,2},{2,0},{4,6},{6,4},{8,10},{10,8},{12,14},{14,12},{16,18},{18,... | collective-permute-start | bytes 786440 | tf_op jit(solution)/shard_map/ppermute | solution.py:300
  62.9 0.0 collective-permute-done.10
  62.9 5.6 %collective-permute-start.12 = (f32[4,128,128]{2,1,0:T(8,128)S(1)}, f32[4,128,128]{2,1,0:T(8,128)S(1)}, u32[]{:S(2)}, u32[]{:S(2)}) collective-permute-start(f32[4,128,128]{2,1,0:T(8,128)S(1)} %get-tuple-element.62.refs_1_), channel_id=1, source_target_pairs={{0,14},{2,4},{4,2},{6,8},{8,6},{10,12},{12,10},{14,0},{16,30},{18,... | collective-permute-start | bytes 786440 | tf_op jit(solution)/shard_map/ppermute | solution.py:310
  68.5 0.0 copy-start.5
  68.6 2.2 %add_cross.8.total_ref = f32[8,128,1024]{2,1,0:T(8,128)S(1)} custom-call(s32[1]{0:T(128)} %bitcast.owner_ref, f32[7]{0:T(128)S(1)} %convert_multiply_fusion.flag_ref, f32[8,128,1024]{2,1,0:T(8,128)S(1)} %add_cross.7.total_ref, bf16[8,1024,128]{2,1,0:T(8,128)(2,1)S(1)} %get-tuple-element.40.q_ref, ...), custom_call_target="tpu_custom_call", output_to_operand_aliasing={{}: (2, {})} | custom-call | flops 1207959552 | bytes 3145728 | tf_op jit(solution)/shard_map/add_cross/pallas_call | solution.py:216
  70.8 0.0 collective-permute-done.9
  70.8 0.0 collective-permute-done.8
  70.8 0.0 collective-permute-done.7.refs_0_
  70.9 0.1 collective-permute-start.14
  71.0 4.9 %collective-permute-start.13 = (f32[4,128,128]{2,1,0:T(8,128)S(1)}, f32[4,128,128]{2,1,0:T(8,128)S(1)}, u32[]{:S(2)}, u32[]{:S(2)}) collective-permute-start(f32[4,128,128]{2,1,0:T(8,128)S(1)} %collective-permute-done.7.refs_0_), channel_id=1, source_target_pairs={{0,2},{2,0},{4,6},{6,4},{8,10},{10,8},{12,14},{14,12},{16,18},{18,... | collective-permute-start | bytes 786440 | tf_op jit(solution)/shard_map/ppermute | solution.py:300
  75.9 0.0 copy-done.5
  75.9 2.0 %finish_own.1.refs_2_ = f32[8192,128]{1,0:T(8,128)S(1)} custom-call(s32[1]{0:T(128)} %bitcast.owner_ref, f32[7]{0:T(128)S(1)} %convert_multiply_fusion.flag_ref, f32[8,128,1024]{2,1,0:T(8,128)S(1)} %add_cross.8.total_ref, bf16[8,1024,128]{2,1,0:T(8,128)(2,1)S(1)} %get-tuple-element.40.q_ref, s32[18,8,1024]{2,1,0:T(8,128)S(1)} %bitcast.12, ...), custom_call_target="tpu_custom_call" | custom-call | flops 536870912 | bytes 4194304 | tf_op jit(solution)/shard_map/finish_own/pallas_call | solution.py:265
  78.0 0.0 collective-permute-done.11.refs_0_
  78.0 0.0 collective-permute-done.12.refs_1_
  78.0 1.9 %add_cross.9.total_ref = f32[8,128,1024]{2,1,0:T(8,128)S(1)} custom-call(s32[1]{0:T(128)} %bitcast.owner_ref, f32[7]{0:T(128)S(1)} %convert_multiply_fusion.flag_ref, f32[8,128,1024]{2,1,0:T(8,128)S(1)} %add_cross.8.total_ref, bf16[8,1024,128]{2,1,0:T(8,128)(2,1)S(1)} %get-tuple-element.40.q_ref, ...), custom_call_target="tpu_custom_call", output_to_operand_aliasing={{}: (2, {})} | custom-call | flops 805306368 | bytes 3145728 | tf_op jit(solution)/shard_map/add_cross/pallas_call | solution.py:216
  79.9 0.0 collective-permute-done.14.refs_1_
  79.9 1.1 %collective-permute-done.13.refs_0_ = f32[4,128,128]{2,1,0:T(8,128)S(1)} collective-permute-done((f32[4,128,128]{2,1,0:T(8,128)S(1)}, f32[4,128,128]{2,1,0:T(8,128)S(1)}, u32[]{:S(2)}, u32[]{:S(2)}) %collective-permute-start.13) | collective-permute-done | bytes 262176 | tf_op jit(solution)/shard_map/ppermute | solution.py:300
  81.0 3.4 %finish_other.1 = (f32[8192,128]{1,0:T(8,128)S(1)}, bf16[8192,128]{1,0:T(8,128)(2,1)}) custom-call(s32[1]{0:T(128)} %bitcast.owner_ref, f32[7]{0:T(128)S(1)} %convert_multiply_fusion.flag_ref, f32[8,128,1024]{2,1,0:T(8,128)S(1)} %add_cross.9.total_ref, bf16[8,1024,128]{2,1,0:T(8,128)(2,1)S(1)} %get-tuple-element.40.q_ref, ...), custom_call_target="tpu_custom_call", output_to_operand_aliasing={{0}: (8, {})} | custom-call | flops 536870912 | bytes 10485760 | tf_op jit(solution)/shard_map/finish_other/pallas_call | solution.py:278
  (7 shorter events, 0.2 us)
Async XLA Ops:
  0.0 6.3 %copy-start.1 = (bf16[1024,8,128]{2,1,0:T(8,128)(2,1)S(1)}, bf16[1024,8,128]{2,1,0:T(8,128)(2,1)}, u32[]{:S(2)}) copy-start(bf16[1024,8,128]{2,1,0:T(8,128)(2,1)} %param.8) | copy-start | bytes 6291460
  0.0 6.3 %copy-start.2 = (bf16[1024,8,128]{2,1,0:T(8,128)(2,1)S(1)}, bf16[1024,8,128]{2,1,0:T(8,128)(2,1)}, u32[]{:S(2)}) copy-start(bf16[1024,8,128]{2,1,0:T(8,128)(2,1)} %param.9) | copy-start | bytes 6291460
  4.3 13.7 %copy-start = (s32[8,18,1024]{2,0,1:T(8,128)S(1)}, s32[8,18,1024]{2,0,1:T(8,128)}, u32[]{:S(2)}) copy-start(s32[8,18,1024]{2,0,1:T(8,128)} %param.10) | copy-start | bytes 1769476
  4.3 8.5 %collective-permute-start = (f32[4,128,128]{2,1,0:T(8,128)}, f32[4,128,128]{2,1,0:T(8,128)S(1)}, u32[]{:S(2)}, u32[]{:S(2)}) collective-permute-start(f32[4,128,128]{2,1,0:T(8,128)} %get-tuple-element.35), channel_id=1, source_target_pairs={{0,2},{2,0},{4,6},{6,4},{8,10},{10,8},{12,14},{14,12},{16,18},{18,... | collective-permute-start | bytes 786440 | tf_op jit(solution)/shard_map/ppermute | solution.py:300
  6.3 1.6 %copy-start.3 = (bf16[1024,8,128]{2,1,0:T(8,128)(2,1)S(1)}, bf16[1024,8,128]{2,1,0:T(8,128)(2,1)}, u32[]{:S(2)}) copy-start(bf16[1024,8,128]{2,1,0:T(8,128)(2,1)} %param.7) | copy-start | bytes 6291460
  7.9 0.9 %copy-start.4 = (f32[4,128,128]{2,1,0:T(8,128)S(1)}, f32[4,128,128]{2,1,0:T(8,128)}, u32[]{:S(2)}) copy-start(f32[4,128,128]{2,1,0:T(8,128)} %get-tuple-element.38._) | copy-start | bytes 786436
  8.8 9.1 %copy-start.6 = (s32[128,128]{1,0:T(8,128)S(1)}, s32[128,128]{1,0:T(8,128)}, u32[]{:S(2)}) copy-start(s32[128,128]{1,0:T(8,128)} %constant.13.clone.map_ref) | copy-start | bytes 196612
  12.8 15.9 %collective-permute-start.1 = (f32[4,128,128]{2,1,0:T(8,128)S(1)}, f32[4,128,128]{2,1,0:T(8,128)S(1)}, u32[]{:S(2)}, u32[]{:S(2)}) collective-permute-start(f32[4,128,128]{2,1,0:T(8,128)S(1)} %copy-done.4), channel_id=1, source_target_pairs={{0,2},{2,0},{4,6},{6,4},{8,10},{10,8},{12,14},{14,12},{16,18},{18,... | collective-permute-start | bytes 786440 | tf_op jit(solution)/shard_map/ppermute | solution.py:300
  14.6 14.2 %collective-permute-start.2 = (f32[4,128,128]{2,1,0:T(8,128)S(1)}, f32[4,128,128]{2,1,0:T(8,128)S(1)}, u32[]{:S(2)}, u32[]{:S(2)}) collective-permute-start(f32[4,128,128]{2,1,0:T(8,128)S(1)} %add.21), channel_id=1, source_target_pairs={{0,4},{2,6},{4,0},{6,2},{8,12},{10,14},{12,8},{14,10},{16,20},{18,... | collective-permute-start | bytes 786440 | tf_op jit(solution)/shard_map/ppermute | solution.py:300
  28.8 13.5 %collective-permute-start.3 = (f32[4,128,128]{2,1,0:T(8,128)S(1)}, f32[4,128,128]{2,1,0:T(8,128)S(1)}, u32[]{:S(2)}, u32[]{:S(2)}) collective-permute-start(f32[4,128,128]{2,1,0:T(8,128)S(1)} %add.22), channel_id=1, source_target_pairs={{0,8},{2,10},{4,12},{6,14},{8,0},{10,2},{12,4},{14,6},{16,24},{18,... | collective-permute-start | bytes 786440 | tf_op jit(solution)/shard_map/ppermute | solution.py:300
  42.4 10.5 %collective-permute-start.6 = (f32[4,128,128]{2,1,0:T(8,128)S(1)}, f32[4,128,128]{2,1,0:T(8,128)S(1)}, u32[]{:S(2)}, u32[]{:S(2)}) collective-permute-start(f32[4,128,128]{2,1,0:T(8,128)S(1)} %add.23), channel_id=1, source_target_pairs={{0,48},{2,50},{4,52},{6,54},{8,56},{10,58},{12,60},{14,62},{16,32}... | collective-permute-start | bytes 786440 | tf_op jit(solution)/shard_map/ppermute | solution.py:300
  42.6 10.3 %collective-permute-start.5 = (f32[4,128,128]{2,1,0:T(8,128)S(1)}, f32[4,128,128]{2,1,0:T(8,128)S(1)}, u32[]{:S(2)}, u32[]{:S(2)}) collective-permute-start(f32[4,128,128]{2,1,0:T(8,128)S(1)} %add.23), channel_id=1, source_target_pairs={{0,32},{2,34},{4,36},{6,38},{8,40},{10,42},{12,44},{14,46},{16,48}... | collective-permute-start | bytes 786440 | tf_op jit(solution)/shard_map/ppermute | solution.py:300
  45.3 8.4 %collective-permute-start.4 = (f32[4,128,128]{2,1,0:T(8,128)S(1)}, f32[4,128,128]{2,1,0:T(8,128)S(1)}, u32[]{:S(2)}, u32[]{:S(2)}) collective-permute-start(f32[4,128,128]{2,1,0:T(8,128)S(1)} %add.23), channel_id=1, source_target_pairs={{0,16},{2,18},{4,20},{6,22},{8,24},{10,26},{12,28},{14,30},{16,0},... | collective-permute-start | bytes 786440 | tf_op jit(solution)/shard_map/ppermute | solution.py:300
  48.4 14.5 %collective-permute-start.10 = (f32[8,128,128]{2,1,0:T(8,128)S(1)}, f32[8,128,128]{2,1,0:T(8,128)S(1)}, u32[]{:S(2)}, u32[]{:S(2)}) collective-permute-start(f32[8,128,128]{2,1,0:T(8,128)S(1)} %pad_maximum_fusion), channel_id=1, source_target_pairs={{0,2},{2,0},{4,6},{6,4},{8,10},{10,8},{12,14},{14,12},{16,18},{18,... | collective-permute-start | bytes 1572872 | tf_op jit(solution)/shard_map/ppermute | solution.py:300
  53.8 17.0 %collective-permute-start.9 = (f32[4,128,128]{2,1,0:T(8,128)S(1)}, f32[4,128,128]{2,1,0:T(8,128)S(1)}, u32[]{:S(2)}, u32[]{:S(2)}) collective-permute-start(f32[4,128,128]{2,1,0:T(8,128)S(1)} %get-tuple-element.65), channel_id=1, source_target_pairs={{0,192},{2,194},{4,196},{6,198},{8,200},{10,202},{12,204},{14,206}... | collective-permute-start | bytes 786440 | tf_op jit(solution)/shard_map/ppermute | solution.py:300
  54.4 16.5 %collective-permute-start.8 = (f32[4,128,128]{2,1,0:T(8,128)S(1)}, f32[4,128,128]{2,1,0:T(8,128)S(1)}, u32[]{:S(2)}, u32[]{:S(2)}) collective-permute-start(f32[4,128,128]{2,1,0:T(8,128)S(1)} %get-tuple-element.65), channel_id=1, source_target_pairs={{0,128},{2,130},{4,132},{6,134},{8,136},{10,138},{12,140},{14,142}... | collective-permute-start | bytes 786440 | tf_op jit(solution)/shard_map/ppermute | solution.py:300
  56.8 14.0 %collective-permute-start.7 = (f32[4,128,128]{2,1,0:T(8,128)S(1)}, f32[4,128,128]{2,1,0:T(8,128)S(1)}, u32[]{:S(2)}, u32[]{:S(2)}) collective-permute-start(f32[4,128,128]{2,1,0:T(8,128)S(1)} %get-tuple-element.65), channel_id=1, source_target_pairs={{0,64},{2,66},{4,68},{6,70},{8,72},{10,74},{12,76},{14,78},{16,80}... | collective-permute-start | bytes 786440 | tf_op jit(solution)/shard_map/ppermute | solution.py:300
  59.8 18.1 %collective-permute-start.11 = (f32[4,128,128]{2,1,0:T(8,128)S(1)}, f32[4,128,128]{2,1,0:T(8,128)S(1)}, u32[]{:S(2)}, u32[]{:S(2)}) collective-permute-start(f32[4,128,128]{2,1,0:T(8,128)S(1)} %collective-permute-done.4.refs_0_), channel_id=1, source_target_pairs={{0,2},{2,0},{4,6},{6,4},{8,10},{10,8},{12,14},{14,12},{16,18},{18,... | collective-permute-start | bytes 786440 | tf_op jit(solution)/shard_map/ppermute | solution.py:300
  62.9 15.1 %collective-permute-start.12 = (f32[4,128,128]{2,1,0:T(8,128)S(1)}, f32[4,128,128]{2,1,0:T(8,128)S(1)}, u32[]{:S(2)}, u32[]{:S(2)}) collective-permute-start(f32[4,128,128]{2,1,0:T(8,128)S(1)} %get-tuple-element.62.refs_1_), channel_id=1, source_target_pairs={{0,14},{2,4},{4,2},{6,8},{8,6},{10,12},{12,10},{14,0},{16,30},{18,... | collective-permute-start | bytes 786440 | tf_op jit(solution)/shard_map/ppermute | solution.py:310
  68.5 7.4 %copy-start.5 = (f32[8,128]{1,0:T(8,128)S(1)}, f32[8,128]{1,0:T(8,128)}, u32[]{:S(2)}) copy-start(f32[8,128]{1,0:T(8,128)} %gain_ref.3) | copy-start | bytes 12292
  70.9 9.0 %collective-permute-start.14 = (f32[4,128,128]{2,1,0:T(8,128)S(1)}, f32[4,128,128]{2,1,0:T(8,128)S(1)}, u32[]{:S(2)}, u32[]{:S(2)}) collective-permute-start(f32[4,128,128]{2,1,0:T(8,128)S(1)} %add.27.refs_1_), channel_id=1, source_target_pairs={{0,14},{2,4},{4,2},{6,8},{8,6},{10,12},{12,10},{14,0},{16,30},{18,... | collective-permute-start | bytes 786440 | tf_op jit(solution)/shard_map/ppermute | solution.py:310
  71.0 10.1 %collective-permute-start.13 = (f32[4,128,128]{2,1,0:T(8,128)S(1)}, f32[4,128,128]{2,1,0:T(8,128)S(1)}, u32[]{:S(2)}, u32[]{:S(2)}) collective-permute-start(f32[4,128,128]{2,1,0:T(8,128)S(1)} %collective-permute-done.7.refs_0_), channel_id=1, source_target_pairs={{0,2},{2,0},{4,6},{6,4},{8,10},{10,8},{12,14},{14,12},{16,18},{18,... | collective-permute-start | bytes 786440 | tf_op jit(solution)/shard_map/ppermute | solution.py:300

commit v3 on v2

--- a/solution.py
+++ b/solution.py
@@ -339,7 +339,7 @@
     total = local(None, True)
     other0, own1, total = lax.optimization_barrier((other0, own1, total))
     block_sum = block_sum + own1
-    own2 = swapped(block_sum, 4)
+    own2 = swapped(block_sum, 6)
     total = local(total, False)
     total = cross(total, True, [own0, own1], (0, 1))
     own2, total = lax.optimization_barrier((own2, total))

time: 84.7 us -> 81.9 us (0.967)
  starting transfers between devices: 37.1 us -> 30.3 us
  waiting for transfers between devices: 11.4 us -> 15.3 us
    ppermute x13, starting transfers between devices: 31.4 us -> 26.9 us  [swapped(): return lax.ppermute(block, 'seq', [(i, i ^ mask) for i in range(count)])]
    ppermute x13, waiting for transfers between devices: 11.3 us -> 14.2 us  [swapped(): return lax.ppermute(block, 'seq', [(i, i ^ mask) for i in range(count)])]
    ppermute x2, starting transfers between devices: 5.68 us -> 3.46 us  [next_along_z(): return lax.ppermute(block, 'seq', route)]
    ppermute x2, waiting for transfers between devices: 0.01 us -> 1.16 us  [next_along_z(): return lax.ppermute(block, 'seq', route)]
  transfers between devices with their start and end apart: 15 -> 15, of which waited for: 6 -> 9; matrix products, arithmetic and copies ran while one was open for 0% -> 0% of each run, Pallas kernels for 30% -> 31%
where the time goes in v3:
time: 81.9 us; the launch traced here: 81.8 us
  Pallas kernels  33 us (40%)
  starting transfers between devices  30.3 us (37%)
  waiting for transfers between devices  15.3 us (19%)
  local copies, waits for them, and re-layouts  2.6 us (3%)
    ppermute x13, starting transfers between devices, swapped(): return lax.ppermute(block, 'seq', [(i, i ^ mask) for i in range(count)])  26.9 us
    ppermute x13, waiting for transfers between devices, swapped(): return lax.ppermute(block, 'seq', [(i, i ^ mask) for i in range(count)])  14.2 us
    pallas_call x2, Pallas kernels, local_part(): pl.pallas_call(functools.partial(local_kernel, length, tile, small, own_h...  10.2 us
    pallas_call x5, Pallas kernels, add_cross(): pl.pallas_call(functools.partial(cross_kernel, bits, first, own_heads), i...  9.71 us
    pallas_call x1, Pallas kernels, make_states(): pl.pallas_call(functools.partial(states_kernel, heads, rows), in_specs=[S...  4.26 us
    ppermute x2, starting transfers between devices, next_along_z(): return lax.ppermute(block, 'seq', route)  3.46 us
    pallas_call x1, Pallas kernels, finish_other(): pl.pallas_call(functools.partial(finish_kernel, bits, first, rows, False)...  3.42 us
    pallas_call x1, Pallas kernels, split_heads(): pl.pallas_call(functools.partial(split_kernel, heads, rows), in_specs=[AN...  3.36 us
  transfers between devices with their start and end apart: 15, of which 9 were waited for; matrix products, arithmetic and copies ran while one was open for 0% of the time, Pallas kernels for 31%

profile of v3, /device:TPU:30, one launch (start us, length us, event | category | flops | bytes accessed | tf_op | source)
XLA Modules:
  0.0 81.8 jit_solution(2087526994780060183)
XLA Ops:
  0.0 0.0 copy-start.1
  0.0 0.0 copy-start.2
  0.0 4.3 %states.1 = (f32[4,128,128]{2,1,0:T(8,128)}, f32[4,128,128]{2,1,0:T(8,128)}) custom-call(s32[1]{0:T(128)} %bitcast.owner_ref, bf16[8192,128]{1,0:T(8,128)(2,1)} %bitcast.15, bf16[8192,128]{1,0:T(8,128)(2,1)} %bitcast.17), custom_call_target="tpu_custom_call" | custom-call | flops 268435456 | bytes 4194304 | tf_op jit(solution)/shard_map/states/pallas_call | solution.py:71
  4.3 0.0 copy-start
  4.3 2.0 %collective-permute-start = (f32[4,128,128]{2,1,0:T(8,128)}, f32[4,128,128]{2,1,0:T(8,128)S(1)}, u32[]{:S(2)}, u32[]{:S(2)}) collective-permute-start(f32[4,128,128]{2,1,0:T(8,128)} %get-tuple-element.35), channel_id=1, source_target_pairs={{0,2},{2,0},{4,6},{6,4},{8,10},{10,8},{12,14},{14,12},{16,18},{18,... | collective-permute-start | bytes 786440 | tf_op jit(solution)/shard_map/ppermute | solution.py:300
  6.3 0.0 copy-done.1
  6.3 0.0 copy-done.2
  6.3 0.0 copy-start.3
  6.3 1.6 %copy-done.3 = bf16[1024,8,128]{2,1,0:T(8,128)(2,1)S(1)} copy-done((bf16[1024,8,128]{2,1,0:T(8,128)(2,1)S(1)}, bf16[1024,8,128]{2,1,0:T(8,128)(2,1)}, u32[]{:S(2)}) %copy-start.3) | copy-done | bytes 2097176
  7.9 0.0 copy-start.4
  7.9 0.9 %copy-done.4 = f32[4,128,128]{2,1,0:T(8,128)S(1)} copy-done((f32[4,128,128]{2,1,0:T(8,128)S(1)}, f32[4,128,128]{2,1,0:T(8,128)}, u32[]{:S(2)}) %copy-start.4) | copy-done | bytes 262168
  8.8 0.0 copy-start.6
  8.8 3.4 %split_heads.1 = (bf16[8,1024,128]{2,1,0:T(8,128)(2,1)S(1)}, bf16[8,1024,128]{2,1,0:T(8,128)(2,1)S(1)}, bf16[8,128,1024]{2,1,0:T(8,128)(2,1)S(1)}) custom-call(f32[4,128,128]{2,1,0:T(8,128)S(1)} %copy-done.4, bf16[8192,128]{1,0:T(8,128)(2,1)S(1)} %bitcast.19, bf16[8192,128]{1,0:T(8,128)(2,1)S(1)} %bitcast.16, bf16[8192,128]{1,0:T(8,128)(2,1)S(1)} %bitcast.18), custom_call_target="tpu_custom_call" | custom-call | bytes 12582912 | tf_op jit(solution)/shard_map/split_heads/pallas_call | solution.py:103
  12.2 0.6 collective-permute-done.refs_0_
  12.8 1.7 %collective-permute-start.1 = (f32[4,128,128]{2,1,0:T(8,128)S(1)}, f32[4,128,128]{2,1,0:T(8,128)S(1)}, u32[]{:S(2)}, u32[]{:S(2)}) collective-permute-start(f32[4,128,128]{2,1,0:T(8,128)S(1)} %copy-done.4), channel_id=1, source_target_pairs={{0,2},{2,0},{4,6},{6,4},{8,10},{10,8},{12,14},{14,12},{16,18},{18,... | collective-permute-start | bytes 786440 | tf_op jit(solution)/shard_map/ppermute | solution.py:300
  14.6 3.4 %collective-permute-start.2 = (f32[4,128,128]{2,1,0:T(8,128)S(1)}, f32[4,128,128]{2,1,0:T(8,128)S(1)}, u32[]{:S(2)}, u32[]{:S(2)}) collective-permute-start(f32[4,128,128]{2,1,0:T(8,128)S(1)} %add.21), channel_id=1, source_target_pairs={{0,4},{2,6},{4,0},{6,2},{8,12},{10,14},{12,8},{14,10},{16,20},{18,... | collective-permute-start | bytes 786440 | tf_op jit(solution)/shard_map/ppermute | solution.py:300
  17.9 0.0 copy-done
  17.9 0.0 copy-done.6
  17.9 5.1 %local_part.2.refs_0_ = f32[8,128,1024]{2,1,0:T(8,128)S(1)} custom-call(s32[1]{0:T(128)} %bitcast.owner_ref, bf16[8,1024,128]{2,1,0:T(8,128)(2,1)S(1)} %get-tuple-element.40.q_ref, bf16[8,1024,128]{2,1,0:T(8,128)(2,1)S(1)} %get-tuple-element.41.k_ref, bf16[8,128,1024]{2,1,0:T(8,128)(2,1)S(1)} %get-tuple-element.42.v_ref, s32[18,8,1024]{2,1,0:T(8,128)S(1)} %bitcast.6, ...), custom_call_target="tpu_custom_call" | custom-call | flops 5368709120 | bytes 8388608 | tf_op jit(solution)/shard_map/local_part/pallas_call | solution.py:172
  23.1 5.7 %collective-permute-done.2.refs_1_ = f32[4,128,128]{2,1,0:T(8,128)S(1)} collective-permute-done((f32[4,128,128]{2,1,0:T(8,128)S(1)}, f32[4,128,128]{2,1,0:T(8,128)S(1)}, u32[]{:S(2)}, u32[]{:S(2)}) %collective-permute-start.2) | collective-permute-done | bytes 262176 | tf_op jit(solution)/shard_map/ppermute | solution.py:300
  28.7 0.0 collective-permute-done.1.refs_0_
  28.8 3.6 %collective-permute-start.3 = (f32[4,128,128]{2,1,0:T(8,128)S(1)}, f32[4,128,128]{2,1,0:T(8,128)S(1)}, u32[]{:S(2)}, u32[]{:S(2)}) collective-permute-start(f32[4,128,128]{2,1,0:T(8,128)S(1)} %add.22), channel_id=1, source_target_pairs={{0,12},{2,14},{4,8},{6,10},{8,4},{10,6},{12,0},{14,2},{16,28},{18,... | collective-permute-start | bytes 786440 | tf_op jit(solution)/shard_map/ppermute | solution.py:300
  32.4 5.1 %local_part.3.total_ref = f32[8,128,1024]{2,1,0:T(8,128)S(1)} custom-call(s32[1]{0:T(128)} %bitcast.owner_ref, bf16[8,1024,128]{2,1,0:T(8,128)(2,1)S(1)} %get-tuple-element.40.q_ref, bf16[8,1024,128]{2,1,0:T(8,128)(2,1)S(1)} %get-tuple-element.41.k_ref, bf16[8,128,1024]{2,1,0:T(8,128)(2,1)S(1)} %get-tuple-element.42.v_ref, ...), custom_call_target="tpu_custom_call", output_to_operand_aliasing={{}: (6, {})} | custom-call | flops 5368709120 | bytes 8388608 | tf_op jit(solution)/shard_map/local_part/pallas_call | solution.py:172
  37.5 1.9 %add_cross.5.total_ref = f32[8,128,1024]{2,1,0:T(8,128)S(1)} custom-call(s32[1]{0:T(128)} %bitcast.owner_ref, f32[7]{0:T(128)S(1)} %convert_multiply_fusion.flag_ref, f32[8,128,1024]{2,1,0:T(8,128)S(1)} %local_part.3.total_ref, bf16[8,1024,128]{2,1,0:T(8,128)(2,1)S(1)} %get-tuple-element.40.q_ref, ...), custom_call_target="tpu_custom_call", output_to_operand_aliasing={{}: (2, {})} | custom-call | flops 805306368 | bytes 3145728 | tf_op jit(solution)/shard_map/add_cross/pallas_call | solution.py:216
  39.4 1.3 %collective-permute-done.3.refs_0_ = f32[4,128,128]{2,1,0:T(8,128)S(1)} collective-permute-done((f32[4,128,128]{2,1,0:T(8,128)S(1)}, f32[4,128,128]{2,1,0:T(8,128)S(1)}, u32[]{:S(2)}, u32[]{:S(2)}) %collective-permute-start.3) | collective-permute-done | bytes 262176 | tf_op jit(solution)/shard_map/ppermute | solution.py:300
  40.7 0.3 collective-permute-start.6
  41.1 2.5 %collective-permute-start.5 = (f32[4,128,128]{2,1,0:T(8,128)S(1)}, f32[4,128,128]{2,1,0:T(8,128)S(1)}, u32[]{:S(2)}, u32[]{:S(2)}) collective-permute-start(f32[4,128,128]{2,1,0:T(8,128)S(1)} %add.23), channel_id=1, source_target_pairs={{0,32},{2,34},{4,36},{6,38},{8,40},{10,42},{12,44},{14,46},{16,48}... | collective-permute-start | bytes 786440 | tf_op jit(solution)/shard_map/ppermute | solution.py:300
  43.6 1.3 %collective-permute-start.4 = (f32[4,128,128]{2,1,0:T(8,128)S(1)}, f32[4,128,128]{2,1,0:T(8,128)S(1)}, u32[]{:S(2)}, u32[]{:S(2)}) collective-permute-start(f32[4,128,128]{2,1,0:T(8,128)S(1)} %add.23), channel_id=1, source_target_pairs={{0,16},{2,18},{4,20},{6,22},{8,24},{10,26},{12,28},{14,30},{16,0},... | collective-permute-start | bytes 786440 | tf_op jit(solution)/shard_map/ppermute | solution.py:300
  44.9 1.8 %add_cross.6.total_ref = f32[8,128,1024]{2,1,0:T(8,128)S(1)} custom-call(s32[1]{0:T(128)} %bitcast.owner_ref, f32[7]{0:T(128)S(1)} %convert_multiply_fusion.flag_ref, f32[8,128,1024]{2,1,0:T(8,128)S(1)} %add_cross.5.total_ref, bf16[8,1024,128]{2,1,0:T(8,128)(2,1)S(1)} %get-tuple-element.40.q_ref, ...), custom_call_target="tpu_custom_call", output_to_operand_aliasing={{}: (2, {})} | custom-call | flops 402653184 | bytes 3145728 | tf_op jit(solution)/shard_map/add_cross/pallas_call | solution.py:216
  46.8 3.0 %collective-permute-start.10 = (f32[8,128,128]{2,1,0:T(8,128)S(1)}, f32[8,128,128]{2,1,0:T(8,128)S(1)}, u32[]{:S(2)}, u32[]{:S(2)}) collective-permute-start(f32[8,128,128]{2,1,0:T(8,128)S(1)} %pad_maximum_fusion), channel_id=1, source_target_pairs={{0,2},{2,0},{4,6},{6,4},{8,10},{10,8},{12,14},{14,12},{16,18},{18,... | collective-permute-start | bytes 1572872 | tf_op jit(solution)/shard_map/ppermute | solution.py:300
  49.7 4.9 %collective-permute-done.6 = f32[4,128,128]{2,1,0:T(8,128)S(1)} collective-permute-done((f32[4,128,128]{2,1,0:T(8,128)S(1)}, f32[4,128,128]{2,1,0:T(8,128)S(1)}, u32[]{:S(2)}, u32[]{:S(2)}) %collective-permute-start.6) | collective-permute-done | bytes 262176 | tf_op jit(solution)/shard_map/ppermute | solution.py:300
  54.6 0.0 collective-permute-done.5
  54.6 0.6 collective-permute-done.4.refs_0_
  55.2 0.1 add_add_fusion
  55.3 0.9 %collective-permute-start.9 = (f32[4,128,128]{2,1,0:T(8,128)S(1)}, f32[4,128,128]{2,1,0:T(8,128)S(1)}, u32[]{:S(2)}, u32[]{:S(2)}) collective-permute-start(f32[4,128,128]{2,1,0:T(8,128)S(1)} %get-tuple-element.65), channel_id=1, source_target_pairs={{0,192},{2,194},{4,196},{6,198},{8,200},{10,202},{12,204},{14,206}... | collective-permute-start | bytes 786440 | tf_op jit(solution)/shard_map/ppermute | solution.py:300
  56.2 2.5 %collective-permute-start.8 = (f32[4,128,128]{2,1,0:T(8,128)S(1)}, f32[4,128,128]{2,1,0:T(8,128)S(1)}, u32[]{:S(2)}, u32[]{:S(2)}) collective-permute-start(f32[4,128,128]{2,1,0:T(8,128)S(1)} %get-tuple-element.65), channel_id=1, source_target_pairs={{0,128},{2,130},{4,132},{6,134},{8,136},{10,138},{12,140},{14,142}... | collective-permute-start | bytes 786440 | tf_op jit(solution)/shard_map/ppermute | solution.py:300
  58.7 0.8 collective-permute-start.7
  59.4 1.9 %add_cross.7.total_ref = f32[8,128,1024]{2,1,0:T(8,128)S(1)} custom-call(s32[1]{0:T(128)} %bitcast.owner_ref, f32[7]{0:T(128)S(1)} %convert_multiply_fusion.flag_ref, f32[8,128,1024]{2,1,0:T(8,128)S(1)} %add_cross.6.total_ref, bf16[8,1024,128]{2,1,0:T(8,128)(2,1)S(1)} %get-tuple-element.40.q_ref, ...), custom_call_target="tpu_custom_call", output_to_operand_aliasing={{}: (2, {})} | custom-call | flops 805306368 | bytes 3145728 | tf_op jit(solution)/shard_map/add_cross/pallas_call | solution.py:216
  61.4 2.8 %collective-permute-start.11 = (f32[4,128,128]{2,1,0:T(8,128)S(1)}, f32[4,128,128]{2,1,0:T(8,128)S(1)}, u32[]{:S(2)}, u32[]{:S(2)}) collective-permute-start(f32[4,128,128]{2,1,0:T(8,128)S(1)} %collective-permute-done.4.refs_0_), channel_id=1, source_target_pairs={{0,2},{2,0},{4,6},{6,4},{8,10},{10,8},{12,14},{14,12},{16,18},{18,... | collective-permute-start | bytes 786440 | tf_op jit(solution)/shard_map/ppermute | solution.py:300
  64.2 0.0 collective-permute-done.10
  64.2 2.6 %collective-permute-start.12 = (f32[4,128,128]{2,1,0:T(8,128)S(1)}, f32[4,128,128]{2,1,0:T(8,128)S(1)}, u32[]{:S(2)}, u32[]{:S(2)}) collective-permute-start(f32[4,128,128]{2,1,0:T(8,128)S(1)} %get-tuple-element.62.refs_1_), channel_id=1, source_target_pairs={{0,14},{2,4},{4,2},{6,8},{8,6},{10,12},{12,10},{14,0},{16,30},{18,... | collective-permute-start | bytes 786440 | tf_op jit(solution)/shard_map/ppermute | solution.py:310
  66.8 0.0 copy-start.5
  66.8 2.2 %add_cross.8.total_ref = f32[8,128,1024]{2,1,0:T(8,128)S(1)} custom-call(s32[1]{0:T(128)} %bitcast.owner_ref, f32[7]{0:T(128)S(1)} %convert_multiply_fusion.flag_ref, f32[8,128,1024]{2,1,0:T(8,128)S(1)} %add_cross.7.total_ref, bf16[8,1024,128]{2,1,0:T(8,128)(2,1)S(1)} %get-tuple-element.40.q_ref, ...), custom_call_target="tpu_custom_call", output_to_operand_aliasing={{}: (2, {})} | custom-call | flops 1207959552 | bytes 3145728 | tf_op jit(solution)/shard_map/add_cross/pallas_call | solution.py:216
  69.0 0.3 collective-permute-done.9
  69.3 0.0 collective-permute-done.8
  69.3 0.6 collective-permute-done.7.refs_0_
  70.0 0.9 %collective-permute-start.14 = (f32[4,128,128]{2,1,0:T(8,128)S(1)}, f32[4,128,128]{2,1,0:T(8,128)S(1)}, u32[]{:S(2)}, u32[]{:S(2)}) collective-permute-start(f32[4,128,128]{2,1,0:T(8,128)S(1)} %add.27.refs_1_), channel_id=1, source_target_pairs={{0,14},{2,4},{4,2},{6,8},{8,6},{10,12},{12,10},{14,0},{16,30},{18,... | collective-permute-start | bytes 786440 | tf_op jit(solution)/shard_map/ppermute | solution.py:310
  70.9 2.0 %collective-permute-start.13 = (f32[4,128,128]{2,1,0:T(8,128)S(1)}, f32[4,128,128]{2,1,0:T(8,128)S(1)}, u32[]{:S(2)}, u32[]{:S(2)}) collective-permute-start(f32[4,128,128]{2,1,0:T(8,128)S(1)} %collective-permute-done.7.refs_0_), channel_id=1, source_target_pairs={{0,2},{2,0},{4,6},{6,4},{8,10},{10,8},{12,14},{14,12},{16,18},{18,... | collective-permute-start | bytes 786440 | tf_op jit(solution)/shard_map/ppermute | solution.py:300
  72.9 0.0 copy-done.5
  72.9 2.0 %finish_own.1.refs_2_ = f32[8192,128]{1,0:T(8,128)S(1)} custom-call(s32[1]{0:T(128)} %bitcast.owner_ref, f32[7]{0:T(128)S(1)} %convert_multiply_fusion.flag_ref, f32[8,128,1024]{2,1,0:T(8,128)S(1)} %add_cross.8.total_ref, bf16[8,1024,128]{2,1,0:T(8,128)(2,1)S(1)} %get-tuple-element.40.q_ref, s32[18,8,1024]{2,1,0:T(8,128)S(1)} %bitcast.12, ...), custom_call_target="tpu_custom_call" | custom-call | flops 536870912 | bytes 4194304 | tf_op jit(solution)/shard_map/finish_own/pallas_call | solution.py:265
  74.9 0.0 collective-permute-done.11.refs_0_
  75.0 0.0 collective-permute-done.12.refs_1_
  75.0 1.9 %add_cross.9.total_ref = f32[8,128,1024]{2,1,0:T(8,128)S(1)} custom-call(s32[1]{0:T(128)} %bitcast.owner_ref, f32[7]{0:T(128)S(1)} %convert_multiply_fusion.flag_ref, f32[8,128,1024]{2,1,0:T(8,128)S(1)} %add_cross.8.total_ref, bf16[8,1024,128]{2,1,0:T(8,128)(2,1)S(1)} %get-tuple-element.40.q_ref, ...), custom_call_target="tpu_custom_call", output_to_operand_aliasing={{}: (2, {})} | custom-call | flops 805306368 | bytes 3145728 | tf_op jit(solution)/shard_map/add_cross/pallas_call | solution.py:216
  76.9 1.2 %collective-permute-done.14.refs_1_ = f32[4,128,128]{2,1,0:T(8,128)S(1)} collective-permute-done((f32[4,128,128]{2,1,0:T(8,128)S(1)}, f32[4,128,128]{2,1,0:T(8,128)S(1)}, u32[]{:S(2)}, u32[]{:S(2)}) %collective-permute-start.14) | collective-permute-done | bytes 262176 | tf_op jit(solution)/shard_map/ppermute | solution.py:310
  78.0 0.2 collective-permute-done.13.refs_0_
  78.2 3.4 %finish_other.1 = (f32[8192,128]{1,0:T(8,128)S(1)}, bf16[8192,128]{1,0:T(8,128)(2,1)}) custom-call(s32[1]{0:T(128)} %bitcast.owner_ref, f32[7]{0:T(128)S(1)} %convert_multiply_fusion.flag_ref, f32[8,128,1024]{2,1,0:T(8,128)S(1)} %add_cross.9.total_ref, bf16[8,1024,128]{2,1,0:T(8,128)(2,1)S(1)} %get-tuple-element.40.q_ref, ...), custom_call_target="tpu_custom_call", output_to_operand_aliasing={{0}: (8, {})} | custom-call | flops 536870912 | bytes 10485760 | tf_op jit(solution)/shard_map/finish_other/pallas_call | solution.py:278
  (7 shorter events, 0.2 us)
Async XLA Ops:
  0.0 6.3 %copy-start.1 = (bf16[1024,8,128]{2,1,0:T(8,128)(2,1)S(1)}, bf16[1024,8,128]{2,1,0:T(8,128)(2,1)}, u32[]{:S(2)}) copy-start(bf16[1024,8,128]{2,1,0:T(8,128)(2,1)} %param.8) | copy-start | bytes 6291460
  0.0 6.3 %copy-start.2 = (bf16[1024,8,128]{2,1,0:T(8,128)(2,1)S(1)}, bf16[1024,8,128]{2,1,0:T(8,128)(2,1)}, u32[]{:S(2)}) copy-start(bf16[1024,8,128]{2,1,0:T(8,128)(2,1)} %param.9) | copy-start | bytes 6291460
  4.3 13.7 %copy-start = (s32[8,18,1024]{2,0,1:T(8,128)S(1)}, s32[8,18,1024]{2,0,1:T(8,128)}, u32[]{:S(2)}) copy-start(s32[8,18,1024]{2,0,1:T(8,128)} %param.10) | copy-start | bytes 1769476
  4.3 8.5 %collective-permute-start = (f32[4,128,128]{2,1,0:T(8,128)}, f32[4,128,128]{2,1,0:T(8,128)S(1)}, u32[]{:S(2)}, u32[]{:S(2)}) collective-permute-start(f32[4,128,128]{2,1,0:T(8,128)} %get-tuple-element.35), channel_id=1, source_target_pairs={{0,2},{2,0},{4,6},{6,4},{8,10},{10,8},{12,14},{14,12},{16,18},{18,... | collective-permute-start | bytes 786440 | tf_op jit(solution)/shard_map/ppermute | solution.py:300
  6.3 1.6 %copy-start.3 = (bf16[1024,8,128]{2,1,0:T(8,128)(2,1)S(1)}, bf16[1024,8,128]{2,1,0:T(8,128)(2,1)}, u32[]{:S(2)}) copy-start(bf16[1024,8,128]{2,1,0:T(8,128)(2,1)} %param.7) | copy-start | bytes 6291460
  7.9 0.9 %copy-start.4 = (f32[4,128,128]{2,1,0:T(8,128)S(1)}, f32[4,128,128]{2,1,0:T(8,128)}, u32[]{:S(2)}) copy-start(f32[4,128,128]{2,1,0:T(8,128)} %get-tuple-element.38._) | copy-start | bytes 786436
  8.8 9.1 %copy-start.6 = (s32[128,128]{1,0:T(8,128)S(1)}, s32[128,128]{1,0:T(8,128)}, u32[]{:S(2)}) copy-start(s32[128,128]{1,0:T(8,128)} %constant.13.clone.map_ref) | copy-start | bytes 196612
  12.8 15.9 %collective-permute-start.1 = (f32[4,128,128]{2,1,0:T(8,128)S(1)}, f32[4,128,128]{2,1,0:T(8,128)S(1)}, u32[]{:S(2)}, u32[]{:S(2)}) collective-permute-start(f32[4,128,128]{2,1,0:T(8,128)S(1)} %copy-done.4), channel_id=1, source_target_pairs={{0,2},{2,0},{4,6},{6,4},{8,10},{10,8},{12,14},{14,12},{16,18},{18,... | collective-permute-start | bytes 786440 | tf_op jit(solution)/shard_map/ppermute | solution.py:300
  14.6 14.2 %collective-permute-start.2 = (f32[4,128,128]{2,1,0:T(8,128)S(1)}, f32[4,128,128]{2,1,0:T(8,128)S(1)}, u32[]{:S(2)}, u32[]{:S(2)}) collective-permute-start(f32[4,128,128]{2,1,0:T(8,128)S(1)} %add.21), channel_id=1, source_target_pairs={{0,4},{2,6},{4,0},{6,2},{8,12},{10,14},{12,8},{14,10},{16,20},{18,... | collective-permute-start | bytes 786440 | tf_op jit(solution)/shard_map/ppermute | solution.py:300
  28.8 11.9 %collective-permute-start.3 = (f32[4,128,128]{2,1,0:T(8,128)S(1)}, f32[4,128,128]{2,1,0:T(8,128)S(1)}, u32[]{:S(2)}, u32[]{:S(2)}) collective-permute-start(f32[4,128,128]{2,1,0:T(8,128)S(1)} %add.22), channel_id=1, source_target_pairs={{0,12},{2,14},{4,8},{6,10},{8,4},{10,6},{12,0},{14,2},{16,28},{18,... | collective-permute-start | bytes 786440 | tf_op jit(solution)/shard_map/ppermute | solution.py:300
  40.7 13.8 %collective-permute-start.6 = (f32[4,128,128]{2,1,0:T(8,128)S(1)}, f32[4,128,128]{2,1,0:T(8,128)S(1)}, u32[]{:S(2)}, u32[]{:S(2)}) collective-permute-start(f32[4,128,128]{2,1,0:T(8,128)S(1)} %add.23), channel_id=1, source_target_pairs={{0,48},{2,50},{4,52},{6,54},{8,56},{10,58},{12,60},{14,62},{16,32}... | collective-permute-start | bytes 786440 | tf_op jit(solution)/shard_map/ppermute | solution.py:300
  41.1 13.5 %collective-permute-start.5 = (f32[4,128,128]{2,1,0:T(8,128)S(1)}, f32[4,128,128]{2,1,0:T(8,128)S(1)}, u32[]{:S(2)}, u32[]{:S(2)}) collective-permute-start(f32[4,128,128]{2,1,0:T(8,128)S(1)} %add.23), channel_id=1, source_target_pairs={{0,32},{2,34},{4,36},{6,38},{8,40},{10,42},{12,44},{14,46},{16,48}... | collective-permute-start | bytes 786440 | tf_op jit(solution)/shard_map/ppermute | solution.py:300
  43.6 11.6 %collective-permute-start.4 = (f32[4,128,128]{2,1,0:T(8,128)S(1)}, f32[4,128,128]{2,1,0:T(8,128)S(1)}, u32[]{:S(2)}, u32[]{:S(2)}) collective-permute-start(f32[4,128,128]{2,1,0:T(8,128)S(1)} %add.23), channel_id=1, source_target_pairs={{0,16},{2,18},{4,20},{6,22},{8,24},{10,26},{12,28},{14,30},{16,0},... | collective-permute-start | bytes 786440 | tf_op jit(solution)/shard_map/ppermute | solution.py:300
  46.8 17.4 %collective-permute-start.10 = (f32[8,128,128]{2,1,0:T(8,128)S(1)}, f32[8,128,128]{2,1,0:T(8,128)S(1)}, u32[]{:S(2)}, u32[]{:S(2)}) collective-permute-start(f32[8,128,128]{2,1,0:T(8,128)S(1)} %pad_maximum_fusion), channel_id=1, source_target_pairs={{0,2},{2,0},{4,6},{6,4},{8,10},{10,8},{12,14},{14,12},{16,18},{18,... | collective-permute-start | bytes 1572872 | tf_op jit(solution)/shard_map/ppermute | solution.py:300
  55.3 14.1 %collective-permute-start.9 = (f32[4,128,128]{2,1,0:T(8,128)S(1)}, f32[4,128,128]{2,1,0:T(8,128)S(1)}, u32[]{:S(2)}, u32[]{:S(2)}) collective-permute-start(f32[4,128,128]{2,1,0:T(8,128)S(1)} %get-tuple-element.65), channel_id=1, source_target_pairs={{0,192},{2,194},{4,196},{6,198},{8,200},{10,202},{12,204},{14,206}... | collective-permute-start | bytes 786440 | tf_op jit(solution)/shard_map/ppermute | solution.py:300
  56.2 13.2 %collective-permute-start.8 = (f32[4,128,128]{2,1,0:T(8,128)S(1)}, f32[4,128,128]{2,1,0:T(8,128)S(1)}, u32[]{:S(2)}, u32[]{:S(2)}) collective-permute-start(f32[4,128,128]{2,1,0:T(8,128)S(1)} %get-tuple-element.65), channel_id=1, source_target_pairs={{0,128},{2,130},{4,132},{6,134},{8,136},{10,138},{12,140},{14,142}... | collective-permute-start | bytes 786440 | tf_op jit(solution)/shard_map/ppermute | solution.py:300
  58.7 11.3 %collective-permute-start.7 = (f32[4,128,128]{2,1,0:T(8,128)S(1)}, f32[4,128,128]{2,1,0:T(8,128)S(1)}, u32[]{:S(2)}, u32[]{:S(2)}) collective-permute-start(f32[4,128,128]{2,1,0:T(8,128)S(1)} %get-tuple-element.65), channel_id=1, source_target_pairs={{0,64},{2,66},{4,68},{6,70},{8,72},{10,74},{12,76},{14,78},{16,80}... | collective-permute-start | bytes 786440 | tf_op jit(solution)/shard_map/ppermute | solution.py:300
  61.4 13.6 %collective-permute-start.11 = (f32[4,128,128]{2,1,0:T(8,128)S(1)}, f32[4,128,128]{2,1,0:T(8,128)S(1)}, u32[]{:S(2)}, u32[]{:S(2)}) collective-permute-start(f32[4,128,128]{2,1,0:T(8,128)S(1)} %collective-permute-done.4.refs_0_), channel_id=1, source_target_pairs={{0,2},{2,0},{4,6},{6,4},{8,10},{10,8},{12,14},{14,12},{16,18},{18,... | collective-permute-start | bytes 786440 | tf_op jit(solution)/shard_map/ppermute | solution.py:300
  64.2 10.8 %collective-permute-start.12 = (f32[4,128,128]{2,1,0:T(8,128)S(1)}, f32[4,128,128]{2,1,0:T(8,128)S(1)}, u32[]{:S(2)}, u32[]{:S(2)}) collective-permute-start(f32[4,128,128]{2,1,0:T(8,128)S(1)} %get-tuple-element.62.refs_1_), channel_id=1, source_target_pairs={{0,14},{2,4},{4,2},{6,8},{8,6},{10,12},{12,10},{14,0},{16,30},{18,... | collective-permute-start | bytes 786440 | tf_op jit(solution)/shard_map/ppermute | solution.py:310
  66.8 6.1 %copy-start.5 = (f32[8,128]{1,0:T(8,128)S(1)}, f32[8,128]{1,0:T(8,128)}, u32[]{:S(2)}) copy-start(f32[8,128]{1,0:T(8,128)} %gain_ref.3) | copy-start | bytes 12292
  70.0 8.0 %collective-permute-start.14 = (f32[4,128,128]{2,1,0:T(8,128)S(1)}, f32[4,128,128]{2,1,0:T(8,128)S(1)}, u32[]{:S(2)}, u32[]{:S(2)}) collective-permute-start(f32[4,128,128]{2,1,0:T(8,128)S(1)} %add.27.refs_1_), channel_id=1, source_target_pairs={{0,14},{2,4},{4,2},{6,8},{8,6},{10,12},{12,10},{14,0},{16,30},{18,... | collective-permute-start | bytes 786440 | tf_op jit(solution)/shard_map/ppermute | solution.py:310
  70.9 7.4 %collective-permute-start.13 = (f32[4,128,128]{2,1,0:T(8,128)S(1)}, f32[4,128,128]{2,1,0:T(8,128)S(1)}, u32[]{:S(2)}, u32[]{:S(2)}) collective-permute-start(f32[4,128,128]{2,1,0:T(8,128)S(1)} %collective-permute-done.7.refs_0_), channel_id=1, source_target_pairs={{0,2},{2,0},{4,6},{6,4},{8,10},{10,8},{12,14},{14,12},{16,18},{18,... | collective-permute-start | bytes 786440 | tf_op jit(solution)/shard_map/ppermute | solution.py:300

commit v4 on v3

--- a/solution.py
+++ b/solution.py
@@ -340,14 +340,15 @@
     other0, own1, total = lax.optimization_barrier((other0, own1, total))
     block_sum = block_sum + own1
     own2 = swapped(block_sum, 6)
+    other1 = swapped(own1, 1)
     total = local(total, False)
     total = cross(total, True, [own0, own1], (0, 1))
-    own2, total = lax.optimization_barrier((own2, total))
+    other1, own2, total = lax.optimization_barrier((other1, own2, total))
     block_sum = block_sum + own2
     own3, left, right = [swapped(block_sum, mask) for mask in (8, 16, 24)]
     total = cross(total, True, [own2], (2,))
-    own1, own2, total = lax.optimization_barrier((own1, own2, total))
-    low = swapped(jnp.concatenate([own1, own2], axis=0), 1)
+    own2, total = lax.optimization_barrier((own2, total))
+    other2 = swapped(own2, 1)
     own3, left, right, total = lax.optimization_barrier((own3, left, right, total))
     own4 = left + right
     block_sum = block_sum + (own3 + own4)
@@ -356,7 +357,7 @@
     own3, own4, total = lax.optimization_barrier((own3, own4, total))
     other3 = swapped(own3, 1)
     other4 = next_along_z(own4)
-    total = cross(total, False, [other0, low[:half], low[half:]], (0, 1, 2))
+    total = cross(total, False, [other0, other1, other2], (0, 1, 2))
     own5, left, right, total = lax.optimization_barrier((own5, left, right, total))
     own6 = left + right
     other5 = swapped(own5, 1)

time: 81.9 us -> 81.8 us (level)
    ppermute x13 -> x14, starting transfers between devices: 26.9 us -> 21.5 us  [swapped(): return lax.ppermute(block, 'seq', [(i, i ^ mask) for i in range(count)])]
    ppermute x2, starting transfers between devices: 3.46 us -> 8.17 us  [next_along_z(): return lax.ppermute(block, 'seq', route)]
    ppermute x13 -> x14, waiting for transfers between devices: 14.2 us -> 14.6 us  [swapped(): return lax.ppermute(block, 'seq', [(i, i ^ mask) for i in range(count)])]
  transfers between devices with their start and end apart: 15 -> 16, of which waited for: 9 -> 7; matrix products, arithmetic and copies ran while one was open for 0% -> 0% of each run, Pallas kernels for 31% -> 31%
where the time goes in v4:
time: 81.8 us; the launch traced here: 81.7 us
  Pallas kernels  33 us (40%)
  starting transfers between devices  29.7 us (36%)
  waiting for transfers between devices  15.9 us (19%)
  local copies, waits for them, and re-layouts  2.56 us (3%)
    ppermute x14, starting transfers between devices, swapped(): return lax.ppermute(block, 'seq', [(i, i ^ mask) for i in range(count)])  21.5 us
    ppermute x14, waiting for transfers between devices, swapped(): return lax.ppermute(block, 'seq', [(i, i ^ mask) for i in range(count)])  14.6 us
    pallas_call x2, Pallas kernels, local_part(): pl.pallas_call(functools.partial(local_kernel, length, tile, small, own_h...  10.2 us
    pallas_call x5, Pallas kernels, add_cross(): pl.pallas_call(functools.partial(cross_kernel, bits, first, own_heads), i...  9.7 us
    ppermute x2, starting transfers between devices, next_along_z(): return lax.ppermute(block, 'seq', route)  8.17 us
    pallas_call x1, Pallas kernels, make_states(): pl.pallas_call(functools.partial(states_kernel, heads, rows), in_specs=[S...  4.26 us
    pallas_call x1, Pallas kernels, finish_other(): pl.pallas_call(functools.partial(finish_kernel, bits, first, rows, False)...  3.4 us
    pallas_call x1, Pallas kernels, split_heads(): pl.pallas_call(functools.partial(split_kernel, heads, rows), in_specs=[AN...  3.36 us
  transfers between devices with their start and end apart: 16, of which 7 were waited for; matrix products, arithmetic and copies ran while one was open for 0% of the time, Pallas kernels for 31%

profile of v4, /device:TPU:30, one launch (start us, length us, event | category | flops | bytes accessed | tf_op | source)
XLA Modules:
  0.0 81.7 jit_solution(9101783018727151943)
XLA Ops:
  0.0 0.0 copy-start.1
  0.0 0.0 copy-start.2
  0.0 4.3 %states.1 = (f32[4,128,128]{2,1,0:T(8,128)}, f32[4,128,128]{2,1,0:T(8,128)}) custom-call(s32[1]{0:T(128)} %bitcast.owner_ref, bf16[8192,128]{1,0:T(8,128)(2,1)} %bitcast.15, bf16[8192,128]{1,0:T(8,128)(2,1)} %bitcast.17), custom_call_target="tpu_custom_call" | custom-call | flops 268435456 | bytes 4194304 | tf_op jit(solution)/shard_map/states/pallas_call | solution.py:71
  4.3 0.0 copy-start
  4.3 2.0 %collective-permute-start = (f32[4,128,128]{2,1,0:T(8,128)}, f32[4,128,128]{2,1,0:T(8,128)S(1)}, u32[]{:S(2)}, u32[]{:S(2)}) collective-permute-start(f32[4,128,128]{2,1,0:T(8,128)} %get-tuple-element.35), channel_id=1, source_target_pairs={{0,2},{2,0},{4,6},{6,4},{8,10},{10,8},{12,14},{14,12},{16,18},{18,... | collective-permute-start | bytes 786440 | tf_op jit(solution)/shard_map/ppermute | solution.py:300
  6.3 0.0 copy-done.1
  6.3 0.0 copy-done.2
  6.3 0.0 copy-start.3
  6.3 1.6 %copy-done.3 = bf16[1024,8,128]{2,1,0:T(8,128)(2,1)S(1)} copy-done((bf16[1024,8,128]{2,1,0:T(8,128)(2,1)S(1)}, bf16[1024,8,128]{2,1,0:T(8,128)(2,1)}, u32[]{:S(2)}) %copy-start.3) | copy-done | bytes 2097176
  7.9 0.0 copy-start.4
  7.9 0.9 %copy-done.4 = f32[4,128,128]{2,1,0:T(8,128)S(1)} copy-done((f32[4,128,128]{2,1,0:T(8,128)S(1)}, f32[4,128,128]{2,1,0:T(8,128)}, u32[]{:S(2)}) %copy-start.4) | copy-done | bytes 262168
  8.8 0.0 copy-start.6
  8.8 3.4 %split_heads.1 = (bf16[8,1024,128]{2,1,0:T(8,128)(2,1)S(1)}, bf16[8,1024,128]{2,1,0:T(8,128)(2,1)S(1)}, bf16[8,128,1024]{2,1,0:T(8,128)(2,1)S(1)}) custom-call(f32[4,128,128]{2,1,0:T(8,128)S(1)} %copy-done.4, bf16[8192,128]{1,0:T(8,128)(2,1)S(1)} %bitcast.19, bf16[8192,128]{1,0:T(8,128)(2,1)S(1)} %bitcast.16, bf16[8192,128]{1,0:T(8,128)(2,1)S(1)} %bitcast.18), custom_call_target="tpu_custom_call" | custom-call | bytes 12582912 | tf_op jit(solution)/shard_map/split_heads/pallas_call | solution.py:103
  12.2 0.6 collective-permute-done.refs_0_
  12.8 1.7 %collective-permute-start.1 = (f32[4,128,128]{2,1,0:T(8,128)S(1)}, f32[4,128,128]{2,1,0:T(8,128)S(1)}, u32[]{:S(2)}, u32[]{:S(2)}) collective-permute-start(f32[4,128,128]{2,1,0:T(8,128)S(1)} %copy-done.4), channel_id=1, source_target_pairs={{0,2},{2,0},{4,6},{6,4},{8,10},{10,8},{12,14},{14,12},{16,18},{18,... | collective-permute-start | bytes 786440 | tf_op jit(solution)/shard_map/ppermute | solution.py:300
  14.6 3.3 %collective-permute-start.2 = (f32[4,128,128]{2,1,0:T(8,128)S(1)}, f32[4,128,128]{2,1,0:T(8,128)S(1)}, u32[]{:S(2)}, u32[]{:S(2)}) collective-permute-start(f32[4,128,128]{2,1,0:T(8,128)S(1)} %add.21), channel_id=1, source_target_pairs={{0,4},{2,6},{4,0},{6,2},{8,12},{10,14},{12,8},{14,10},{16,20},{18,... | collective-permute-start | bytes 786440 | tf_op jit(solution)/shard_map/ppermute | solution.py:300
  17.9 0.0 copy-done
  17.9 0.0 copy-done.6
  18.0 5.1 %local_part.2.refs_0_ = f32[8,128,1024]{2,1,0:T(8,128)S(1)} custom-call(s32[1]{0:T(128)} %bitcast.owner_ref, bf16[8,1024,128]{2,1,0:T(8,128)(2,1)S(1)} %get-tuple-element.40.q_ref, bf16[8,1024,128]{2,1,0:T(8,128)(2,1)S(1)} %get-tuple-element.41.k_ref, bf16[8,128,1024]{2,1,0:T(8,128)(2,1)S(1)} %get-tuple-element.42.v_ref, s32[18,8,1024]{2,1,0:T(8,128)S(1)} %bitcast.6, ...), custom_call_target="tpu_custom_call" | custom-call | flops 5368709120 | bytes 8388608 | tf_op jit(solution)/shard_map/local_part/pallas_call | solution.py:172
  23.1 5.8 %collective-permute-done.2.refs_1_ = f32[4,128,128]{2,1,0:T(8,128)S(1)} collective-permute-done((f32[4,128,128]{2,1,0:T(8,128)S(1)}, f32[4,128,128]{2,1,0:T(8,128)S(1)}, u32[]{:S(2)}, u32[]{:S(2)}) %collective-permute-start.2) | collective-permute-done | bytes 262176 | tf_op jit(solution)/shard_map/ppermute | solution.py:300
  28.9 0.0 collective-permute-done.1.refs_0_
  28.9 0.4 collective-permute-start.3
  29.3 5.5 %collective-permute-start.4 = (f32[4,128,128]{2,1,0:T(8,128)S(1)}, f32[4,128,128]{2,1,0:T(8,128)S(1)}, u32[]{:S(2)}, u32[]{:S(2)}) collective-permute-start(f32[4,128,128]{2,1,0:T(8,128)S(1)} %add.22), channel_id=1, source_target_pairs={{0,12},{2,14},{4,8},{6,10},{8,4},{10,6},{12,0},{14,2},{16,28},{18,... | collective-permute-start | bytes 786440 | tf_op jit(solution)/shard_map/ppermute | solution.py:300
  34.8 5.1 %local_part.3.total_ref = f32[8,128,1024]{2,1,0:T(8,128)S(1)} custom-call(s32[1]{0:T(128)} %bitcast.owner_ref, bf16[8,1024,128]{2,1,0:T(8,128)(2,1)S(1)} %get-tuple-element.40.q_ref, bf16[8,1024,128]{2,1,0:T(8,128)(2,1)S(1)} %get-tuple-element.41.k_ref, bf16[8,128,1024]{2,1,0:T(8,128)(2,1)S(1)} %get-tuple-element.42.v_ref, ...), custom_call_target="tpu_custom_call", output_to_operand_aliasing={{}: (6, {})} | custom-call | flops 5368709120 | bytes 8388608 | tf_op jit(solution)/shard_map/local_part/pallas_call | solution.py:172
  39.9 1.9 %add_cross.5.total_ref = f32[8,128,1024]{2,1,0:T(8,128)S(1)} custom-call(s32[1]{0:T(128)} %bitcast.owner_ref, f32[7]{0:T(128)S(1)} %convert_multiply_fusion.flag_ref, f32[8,128,1024]{2,1,0:T(8,128)S(1)} %local_part.3.total_ref, bf16[8,1024,128]{2,1,0:T(8,128)(2,1)S(1)} %get-tuple-element.40.q_ref, ...), custom_call_target="tpu_custom_call", output_to_operand_aliasing={{}: (2, {})} | custom-call | flops 805306368 | bytes 3145728 | tf_op jit(solution)/shard_map/add_cross/pallas_call | solution.py:216
  41.8 1.5 %collective-permute-done.4.refs_0_ = f32[4,128,128]{2,1,0:T(8,128)S(1)} collective-permute-done((f32[4,128,128]{2,1,0:T(8,128)S(1)}, f32[4,128,128]{2,1,0:T(8,128)S(1)}, u32[]{:S(2)}, u32[]{:S(2)}) %collective-permute-start.4) | collective-permute-done | bytes 262176 | tf_op jit(solution)/shard_map/ppermute | solution.py:300
  43.3 0.0 collective-permute-done.3.refs_1_
  43.3 0.3 collective-permute-start.7
  43.6 2.6 %collective-permute-start.6 = (f32[4,128,128]{2,1,0:T(8,128)S(1)}, f32[4,128,128]{2,1,0:T(8,128)S(1)}, u32[]{:S(2)}, u32[]{:S(2)}) collective-permute-start(f32[4,128,128]{2,1,0:T(8,128)S(1)} %add.23), channel_id=1, source_target_pairs={{0,32},{2,34},{4,36},{6,38},{8,40},{10,42},{12,44},{14,46},{16,48}... | collective-permute-start | bytes 786440 | tf_op jit(solution)/shard_map/ppermute | solution.py:300
  46.2 1.3 %collective-permute-start.5 = (f32[4,128,128]{2,1,0:T(8,128)S(1)}, f32[4,128,128]{2,1,0:T(8,128)S(1)}, u32[]{:S(2)}, u32[]{:S(2)}) collective-permute-start(f32[4,128,128]{2,1,0:T(8,128)S(1)} %add.23), channel_id=1, source_target_pairs={{0,16},{2,18},{4,20},{6,22},{8,24},{10,26},{12,28},{14,30},{16,0},... | collective-permute-start | bytes 786440 | tf_op jit(solution)/shard_map/ppermute | solution.py:300
  47.5 1.8 %add_cross.6.total_ref = f32[8,128,1024]{2,1,0:T(8,128)S(1)} custom-call(s32[1]{0:T(128)} %bitcast.owner_ref, f32[7]{0:T(128)S(1)} %convert_multiply_fusion.flag_ref, f32[8,128,1024]{2,1,0:T(8,128)S(1)} %add_cross.5.total_ref, bf16[8,1024,128]{2,1,0:T(8,128)(2,1)S(1)} %get-tuple-element.40.q_ref, ...), custom_call_target="tpu_custom_call", output_to_operand_aliasing={{}: (2, {})} | custom-call | flops 402653184 | bytes 3145728 | tf_op jit(solution)/shard_map/add_cross/pallas_call | solution.py:216
  49.3 0.1 collective-permute-start.11
  49.4 4.5 %collective-permute-done.7 = f32[4,128,128]{2,1,0:T(8,128)S(1)} collective-permute-done((f32[4,128,128]{2,1,0:T(8,128)S(1)}, f32[4,128,128]{2,1,0:T(8,128)S(1)}, u32[]{:S(2)}, u32[]{:S(2)}) %collective-permute-start.7) | collective-permute-done | bytes 262176 | tf_op jit(solution)/shard_map/ppermute | solution.py:300
  53.9 0.0 collective-permute-done.6
  53.9 0.7 collective-permute-done.5.refs_0_
  54.7 0.1 add_add_fusion
  54.7 0.6 collective-permute-start.10
  55.3 2.4 %collective-permute-start.9 = (f32[4,128,128]{2,1,0:T(8,128)S(1)}, f32[4,128,128]{2,1,0:T(8,128)S(1)}, u32[]{:S(2)}, u32[]{:S(2)}) collective-permute-start(f32[4,128,128]{2,1,0:T(8,128)S(1)} %get-tuple-element.65), channel_id=1, source_target_pairs={{0,128},{2,130},{4,132},{6,134},{8,136},{10,138},{12,140},{14,142}... | collective-permute-start | bytes 786440 | tf_op jit(solution)/shard_map/ppermute | solution.py:300
  57.7 1.2 %collective-permute-start.8 = (f32[4,128,128]{2,1,0:T(8,128)S(1)}, f32[4,128,128]{2,1,0:T(8,128)S(1)}, u32[]{:S(2)}, u32[]{:S(2)}) collective-permute-start(f32[4,128,128]{2,1,0:T(8,128)S(1)} %get-tuple-element.65), channel_id=1, source_target_pairs={{0,64},{2,66},{4,68},{6,70},{8,72},{10,74},{12,76},{14,78},{16,80}... | collective-permute-start | bytes 786440 | tf_op jit(solution)/shard_map/ppermute | solution.py:300
  58.9 1.9 %add_cross.7.total_ref = f32[8,128,1024]{2,1,0:T(8,128)S(1)} custom-call(s32[1]{0:T(128)} %bitcast.owner_ref, f32[7]{0:T(128)S(1)} %convert_multiply_fusion.flag_ref, f32[8,128,1024]{2,1,0:T(8,128)S(1)} %add_cross.6.total_ref, bf16[8,1024,128]{2,1,0:T(8,128)(2,1)S(1)} %get-tuple-element.40.q_ref, ...), custom_call_target="tpu_custom_call", output_to_operand_aliasing={{}: (2, {})} | custom-call | flops 805306368 | bytes 3145728 | tf_op jit(solution)/shard_map/add_cross/pallas_call | solution.py:216
  60.8 0.0 copy-start.5
  60.8 0.1 collective-permute-start.12
  60.9 0.0 collective-permute-done.11.refs_2_
  60.9 4.0 %collective-permute-start.13 = (f32[4,128,128]{2,1,0:T(8,128)S(1)}, f32[4,128,128]{2,1,0:T(8,128)S(1)}, u32[]{:S(2)}, u32[]{:S(2)}) collective-permute-start(f32[4,128,128]{2,1,0:T(8,128)S(1)} %get-tuple-element.62.refs_1_), channel_id=1, source_target_pairs={{0,14},{2,4},{4,2},{6,8},{8,6},{10,12},{12,10},{14,0},{16,30},{18,... | collective-permute-start | bytes 786440 | tf_op jit(solution)/shard_map/ppermute | solution.py:310
  65.0 2.2 %add_cross.8.total_ref = f32[8,128,1024]{2,1,0:T(8,128)S(1)} custom-call(s32[1]{0:T(128)} %bitcast.owner_ref, f32[7]{0:T(128)S(1)} %convert_multiply_fusion.flag_ref, f32[8,128,1024]{2,1,0:T(8,128)S(1)} %add_cross.7.total_ref, bf16[8,1024,128]{2,1,0:T(8,128)(2,1)S(1)} %get-tuple-element.40.q_ref, ...), custom_call_target="tpu_custom_call", output_to_operand_aliasing={{}: (2, {})} | custom-call | flops 1207959552 | bytes 3145728 | tf_op jit(solution)/shard_map/add_cross/pallas_call | solution.py:216
  67.2 0.0 collective-permute-done.10
  67.2 0.0 collective-permute-done.9
  67.2 0.0 collective-permute-done.8.refs_0_
  67.3 4.1 %collective-permute-start.15 = (f32[4,128,128]{2,1,0:T(8,128)S(1)}, f32[4,128,128]{2,1,0:T(8,128)S(1)}, u32[]{:S(2)}, u32[]{:S(2)}) collective-permute-start(f32[4,128,128]{2,1,0:T(8,128)S(1)} %add.27.refs_1_), channel_id=1, source_target_pairs={{0,14},{2,4},{4,2},{6,8},{8,6},{10,12},{12,10},{14,0},{16,30},{18,... | collective-permute-start | bytes 786440 | tf_op jit(solution)/shard_map/ppermute | solution.py:310
  71.4 0.0 collective-permute-start.14
  71.4 0.0 copy-done.5
  71.4 2.0 %finish_own.1.refs_2_ = f32[8192,128]{1,0:T(8,128)S(1)} custom-call(s32[1]{0:T(128)} %bitcast.owner_ref, f32[7]{0:T(128)S(1)} %convert_multiply_fusion.flag_ref, f32[8,128,1024]{2,1,0:T(8,128)S(1)} %add_cross.8.total_ref, bf16[8,1024,128]{2,1,0:T(8,128)(2,1)S(1)} %get-tuple-element.40.q_ref, s32[18,8,1024]{2,1,0:T(8,128)S(1)} %bitcast.12, ...), custom_call_target="tpu_custom_call" | custom-call | flops 536870912 | bytes 4194304 | tf_op jit(solution)/shard_map/finish_own/pallas_call | solution.py:265
  73.5 0.0 collective-permute-done.12.refs_0_
  73.5 0.0 collective-permute-done.13.refs_1_
  73.5 1.9 %add_cross.9.total_ref = f32[8,128,1024]{2,1,0:T(8,128)S(1)} custom-call(s32[1]{0:T(128)} %bitcast.owner_ref, f32[7]{0:T(128)S(1)} %convert_multiply_fusion.flag_ref, f32[8,128,1024]{2,1,0:T(8,128)S(1)} %add_cross.8.total_ref, bf16[8,1024,128]{2,1,0:T(8,128)(2,1)S(1)} %get-tuple-element.40.q_ref, ...), custom_call_target="tpu_custom_call", output_to_operand_aliasing={{}: (2, {})} | custom-call | flops 805306368 | bytes 3145728 | tf_op jit(solution)/shard_map/add_cross/pallas_call | solution.py:216
  75.4 1.3 %collective-permute-done.15.refs_1_ = f32[4,128,128]{2,1,0:T(8,128)S(1)} collective-permute-done((f32[4,128,128]{2,1,0:T(8,128)S(1)}, f32[4,128,128]{2,1,0:T(8,128)S(1)}, u32[]{:S(2)}, u32[]{:S(2)}) %collective-permute-start.15) | collective-permute-done | bytes 262176 | tf_op jit(solution)/shard_map/ppermute | solution.py:310
  76.7 1.5 %collective-permute-done.14.refs_0_ = f32[4,128,128]{2,1,0:T(8,128)S(1)} collective-permute-done((f32[4,128,128]{2,1,0:T(8,128)S(1)}, f32[4,128,128]{2,1,0:T(8,128)S(1)}, u32[]{:S(2)}, u32[]{:S(2)}) %collective-permute-start.14) | collective-permute-done | bytes 262176 | tf_op jit(solution)/shard_map/ppermute | solution.py:300
  78.1 3.4 %finish_other.1 = (f32[8192,128]{1,0:T(8,128)S(1)}, bf16[8192,128]{1,0:T(8,128)(2,1)}) custom-call(s32[1]{0:T(128)} %bitcast.owner_ref, f32[7]{0:T(128)S(1)} %convert_multiply_fusion.flag_ref, f32[8,128,1024]{2,1,0:T(8,128)S(1)} %add_cross.9.total_ref, bf16[8,1024,128]{2,1,0:T(8,128)(2,1)S(1)} %get-tuple-element.40.q_ref, ...), custom_call_target="tpu_custom_call", output_to_operand_aliasing={{0}: (8, {})} | custom-call | flops 536870912 | bytes 10485760 | tf_op jit(solution)/shard_map/finish_other/pallas_call | solution.py:278
  (5 shorter events, 0.1 us)
Async XLA Ops:
  0.0 6.3 %copy-start.1 = (bf16[1024,8,128]{2,1,0:T(8,128)(2,1)S(1)}, bf16[1024,8,128]{2,1,0:T(8,128)(2,1)}, u32[]{:S(2)}) copy-start(bf16[1024,8,128]{2,1,0:T(8,128)(2,1)} %param.8) | copy-start | bytes 6291460
  0.0 6.3 %copy-start.2 = (bf16[1024,8,128]{2,1,0:T(8,128)(2,1)S(1)}, bf16[1024,8,128]{2,1,0:T(8,128)(2,1)}, u32[]{:S(2)}) copy-start(bf16[1024,8,128]{2,1,0:T(8,128)(2,1)} %param.9) | copy-start | bytes 6291460
  4.3 13.7 %copy-start = (s32[8,18,1024]{2,0,1:T(8,128)S(1)}, s32[8,18,1024]{2,0,1:T(8,128)}, u32[]{:S(2)}) copy-start(s32[8,18,1024]{2,0,1:T(8,128)} %param.10) | copy-start | bytes 1769476
  4.3 8.5 %collective-permute-start = (f32[4,128,128]{2,1,0:T(8,128)}, f32[4,128,128]{2,1,0:T(8,128)S(1)}, u32[]{:S(2)}, u32[]{:S(2)}) collective-permute-start(f32[4,128,128]{2,1,0:T(8,128)} %get-tuple-element.35), channel_id=1, source_target_pairs={{0,2},{2,0},{4,6},{6,4},{8,10},{10,8},{12,14},{14,12},{16,18},{18,... | collective-permute-start | bytes 786440 | tf_op jit(solution)/shard_map/ppermute | solution.py:300
  6.3 1.6 %copy-start.3 = (bf16[1024,8,128]{2,1,0:T(8,128)(2,1)S(1)}, bf16[1024,8,128]{2,1,0:T(8,128)(2,1)}, u32[]{:S(2)}) copy-start(bf16[1024,8,128]{2,1,0:T(8,128)(2,1)} %param.7) | copy-start | bytes 6291460
  7.9 0.9 %copy-start.4 = (f32[4,128,128]{2,1,0:T(8,128)S(1)}, f32[4,128,128]{2,1,0:T(8,128)}, u32[]{:S(2)}) copy-start(f32[4,128,128]{2,1,0:T(8,128)} %get-tuple-element.38._) | copy-start | bytes 786436
  8.8 9.1 %copy-start.6 = (s32[128,128]{1,0:T(8,128)S(1)}, s32[128,128]{1,0:T(8,128)}, u32[]{:S(2)}) copy-start(s32[128,128]{1,0:T(8,128)} %constant.13.clone.map_ref) | copy-start | bytes 196612
  12.8 16.1 %collective-permute-start.1 = (f32[4,128,128]{2,1,0:T(8,128)S(1)}, f32[4,128,128]{2,1,0:T(8,128)S(1)}, u32[]{:S(2)}, u32[]{:S(2)}) collective-permute-start(f32[4,128,128]{2,1,0:T(8,128)S(1)} %copy-done.4), channel_id=1, source_target_pairs={{0,2},{2,0},{4,6},{6,4},{8,10},{10,8},{12,14},{14,12},{16,18},{18,... | collective-permute-start | bytes 786440 | tf_op jit(solution)/shard_map/ppermute | solution.py:300
  14.6 14.3 %collective-permute-start.2 = (f32[4,128,128]{2,1,0:T(8,128)S(1)}, f32[4,128,128]{2,1,0:T(8,128)S(1)}, u32[]{:S(2)}, u32[]{:S(2)}) collective-permute-start(f32[4,128,128]{2,1,0:T(8,128)S(1)} %add.21), channel_id=1, source_target_pairs={{0,4},{2,6},{4,0},{6,2},{8,12},{10,14},{12,8},{14,10},{16,20},{18,... | collective-permute-start | bytes 786440 | tf_op jit(solution)/shard_map/ppermute | solution.py:300
  28.9 14.4 %collective-permute-start.3 = (f32[4,128,128]{2,1,0:T(8,128)S(1)}, f32[4,128,128]{2,1,0:T(8,128)S(1)}, u32[]{:S(2)}, u32[]{:S(2)}) collective-permute-start(f32[4,128,128]{2,1,0:T(8,128)S(1)} %collective-permute-done.2.refs_1_), channel_id=1, source_target_pairs={{0,2},{2,0},{4,6},{6,4},{8,10},{10,8},{12,14},{14,12},{16,18},{18,... | collective-permute-start | bytes 786440 | tf_op jit(solution)/shard_map/ppermute | solution.py:300
  29.3 14.0 %collective-permute-start.4 = (f32[4,128,128]{2,1,0:T(8,128)S(1)}, f32[4,128,128]{2,1,0:T(8,128)S(1)}, u32[]{:S(2)}, u32[]{:S(2)}) collective-permute-start(f32[4,128,128]{2,1,0:T(8,128)S(1)} %add.22), channel_id=1, source_target_pairs={{0,12},{2,14},{4,8},{6,10},{8,4},{10,6},{12,0},{14,2},{16,28},{18,... | collective-permute-start | bytes 786440 | tf_op jit(solution)/shard_map/ppermute | solution.py:300
  43.3 10.6 %collective-permute-start.7 = (f32[4,128,128]{2,1,0:T(8,128)S(1)}, f32[4,128,128]{2,1,0:T(8,128)S(1)}, u32[]{:S(2)}, u32[]{:S(2)}) collective-permute-start(f32[4,128,128]{2,1,0:T(8,128)S(1)} %add.23), channel_id=1, source_target_pairs={{0,48},{2,50},{4,52},{6,54},{8,56},{10,58},{12,60},{14,62},{16,32}... | collective-permute-start | bytes 786440 | tf_op jit(solution)/shard_map/ppermute | solution.py:300
  43.6 10.3 %collective-permute-start.6 = (f32[4,128,128]{2,1,0:T(8,128)S(1)}, f32[4,128,128]{2,1,0:T(8,128)S(1)}, u32[]{:S(2)}, u32[]{:S(2)}) collective-permute-start(f32[4,128,128]{2,1,0:T(8,128)S(1)} %add.23), channel_id=1, source_target_pairs={{0,32},{2,34},{4,36},{6,38},{8,40},{10,42},{12,44},{14,46},{16,48}... | collective-permute-start | bytes 786440 | tf_op jit(solution)/shard_map/ppermute | solution.py:300
  46.2 8.4 %collective-permute-start.5 = (f32[4,128,128]{2,1,0:T(8,128)S(1)}, f32[4,128,128]{2,1,0:T(8,128)S(1)}, u32[]{:S(2)}, u32[]{:S(2)}) collective-permute-start(f32[4,128,128]{2,1,0:T(8,128)S(1)} %add.23), channel_id=1, source_target_pairs={{0,16},{2,18},{4,20},{6,22},{8,24},{10,26},{12,28},{14,30},{16,0},... | collective-permute-start | bytes 786440 | tf_op jit(solution)/shard_map/ppermute | solution.py:300
  49.3 11.6 %collective-permute-start.11 = (f32[4,128,128]{2,1,0:T(8,128)S(1)}, f32[4,128,128]{2,1,0:T(8,128)S(1)}, u32[]{:S(2)}, u32[]{:S(2)}) collective-permute-start(f32[4,128,128]{2,1,0:T(8,128)S(1)} %collective-permute-done.4.refs_0_), channel_id=1, source_target_pairs={{0,2},{2,0},{4,6},{6,4},{8,10},{10,8},{12,14},{14,12},{16,18},{18,... | collective-permute-start | bytes 786440 | tf_op jit(solution)/shard_map/ppermute | solution.py:300
  54.7 12.5 %collective-permute-start.10 = (f32[4,128,128]{2,1,0:T(8,128)S(1)}, f32[4,128,128]{2,1,0:T(8,128)S(1)}, u32[]{:S(2)}, u32[]{:S(2)}) collective-permute-start(f32[4,128,128]{2,1,0:T(8,128)S(1)} %get-tuple-element.65), channel_id=1, source_target_pairs={{0,192},{2,194},{4,196},{6,198},{8,200},{10,202},{12,204},{14,206}... | collective-permute-start | bytes 786440 | tf_op jit(solution)/shard_map/ppermute | solution.py:300
  55.3 11.9 %collective-permute-start.9 = (f32[4,128,128]{2,1,0:T(8,128)S(1)}, f32[4,128,128]{2,1,0:T(8,128)S(1)}, u32[]{:S(2)}, u32[]{:S(2)}) collective-permute-start(f32[4,128,128]{2,1,0:T(8,128)S(1)} %get-tuple-element.65), channel_id=1, source_target_pairs={{0,128},{2,130},{4,132},{6,134},{8,136},{10,138},{12,140},{14,142}... | collective-permute-start | bytes 786440 | tf_op jit(solution)/shard_map/ppermute | solution.py:300
  57.7 9.5 %collective-permute-start.8 = (f32[4,128,128]{2,1,0:T(8,128)S(1)}, f32[4,128,128]{2,1,0:T(8,128)S(1)}, u32[]{:S(2)}, u32[]{:S(2)}) collective-permute-start(f32[4,128,128]{2,1,0:T(8,128)S(1)} %get-tuple-element.65), channel_id=1, source_target_pairs={{0,64},{2,66},{4,68},{6,70},{8,72},{10,74},{12,76},{14,78},{16,80}... | collective-permute-start | bytes 786440 | tf_op jit(solution)/shard_map/ppermute | solution.py:300
  60.8 10.6 %copy-start.5 = (f32[8,128]{1,0:T(8,128)S(1)}, f32[8,128]{1,0:T(8,128)}, u32[]{:S(2)}) copy-start(f32[8,128]{1,0:T(8,128)} %gain_ref.3) | copy-start | bytes 12292
  60.8 12.6 %collective-permute-start.12 = (f32[4,128,128]{2,1,0:T(8,128)S(1)}, f32[4,128,128]{2,1,0:T(8,128)S(1)}, u32[]{:S(2)}, u32[]{:S(2)}) collective-permute-start(f32[4,128,128]{2,1,0:T(8,128)S(1)} %collective-permute-done.5.refs_0_), channel_id=1, source_target_pairs={{0,2},{2,0},{4,6},{6,4},{8,10},{10,8},{12,14},{14,12},{16,18},{18,... | collective-permute-start | bytes 786440 | tf_op jit(solution)/shard_map/ppermute | solution.py:300
  60.9 12.5 %collective-permute-start.13 = (f32[4,128,128]{2,1,0:T(8,128)S(1)}, f32[4,128,128]{2,1,0:T(8,128)S(1)}, u32[]{:S(2)}, u32[]{:S(2)}) collective-permute-start(f32[4,128,128]{2,1,0:T(8,128)S(1)} %get-tuple-element.62.refs_1_), channel_id=1, source_target_pairs={{0,14},{2,4},{4,2},{6,8},{8,6},{10,12},{12,10},{14,0},{16,30},{18,... | collective-permute-start | bytes 786440 | tf_op jit(solution)/shard_map/ppermute | solution.py:310
  67.3 9.4 %collective-permute-start.15 = (f32[4,128,128]{2,1,0:T(8,128)S(1)}, f32[4,128,128]{2,1,0:T(8,128)S(1)}, u32[]{:S(2)}, u32[]{:S(2)}) collective-permute-start(f32[4,128,128]{2,1,0:T(8,128)S(1)} %add.27.refs_1_), channel_id=1, source_target_pairs={{0,14},{2,4},{4,2},{6,8},{8,6},{10,12},{12,10},{14,0},{16,30},{18,... | collective-permute-start | bytes 786440 | tf_op jit(solution)/shard_map/ppermute | solution.py:310
  71.4 6.7 %collective-permute-start.14 = (f32[4,128,128]{2,1,0:T(8,128)S(1)}, f32[4,128,128]{2,1,0:T(8,128)S(1)}, u32[]{:S(2)}, u32[]{:S(2)}) collective-permute-start(f32[4,128,128]{2,1,0:T(8,128)S(1)} %collective-permute-done.8.refs_0_), channel_id=1, source_target_pairs={{0,2},{2,0},{4,6},{6,4},{8,10},{10,8},{12,14},{14,12},{16,18},{18,... | collective-permute-start | bytes 786440 | tf_op jit(solution)/shard_map/ppermute | solution.py:300
